TPU v7x, 32 devices: a whole 2x2x4 slice. The times are simulated.
32 devices in a mesh: row: 2 (over core), col: 16 (over z, y, x).
Axes of the slice: x: 2, y: 2, z: 4, core: 2. Of those that a mesh axis runs over, the one named last changes fastest.
Arguments:
- features: bfloat16 [16384, 128], P(('row', 'col')), may hold values from -6 to 6
- weight: bfloat16 [128, 128], replicated, may hold values from -0.5 to 0.5
- bias: float32 [128], replicated, may hold values from -3 to 3
- cotangent: bfloat16 [16384, 128], P(('row', 'col')), may hold values from -6 to 6
- block_count: int32 [2, 16], P('row', 'col'), may hold values from 64 to 512
- block_rows: int32 [2, 16, 512], P('row', 'col'), may hold values from 0 to 63
- block_cols: int32 [2, 16, 512], P('row', 'col'), may hold values from 0 to 7
- edge_offsets: int32 [2, 16, 512, 128], P('row', 'col'), may hold values from 0 to 16383, as said below
- edge_weight: bfloat16 [2, 16, 512, 128], P('row', 'col'), may hold values from 0.0099487305 to 0.099609375
Outputs:
- output: bfloat16 [16384, 128], P(('row', 'col'))
- grad_features: bfloat16 [16384, 128], P(('row', 'col'))
- grad_weight: float32 [128, 128], replicated
- grad_bias: float32 [128], replicated
Inputs may be any that keep to these rules, and one draw needn't show every extreme that they name: `edge_offsets`: the offsets within one slot are distinct.
All inputs are finite; a program needn't handle non-finite values.
Results may differ from a plain program's by a relative error of at most 0.013.
The roundings to bfloat16 on the way count: a program that leaves them out, or rounds other values in their place, can miss the bound.
Values may be sent and summed in bfloat16 or wider, within the bound.
No kernel may reach another device: no remote copies, remote signals or barrier semaphores. Data moves between devices by JAX's collectives and lax.ppermute only.
A program may use at most 128 MiB of HBM per device.

v0:
```python
import functools
import functools
import jax
import jax.numpy as jnp
from jax import lax
from jax.experimental import pallas as pl
from jax.experimental.pallas import tpu as pltpu
from jax.experimental.layout import Layout, with_layout_constraint
from jax.sharding import PartitionSpec as P


def swap(x, axis, bit):
    n = lax.axis_size(axis)
    return lax.ppermute(x, axis, [(i, i ^ bit) for i in range(n)])


def bits_of(axis):
    n = lax.axis_size(axis)
    return [1 << k for k in range(n.bit_length() - 1)]


def scatter_sum(x, axis):
    for bit in bits_of(axis):
        pairs = x.reshape((x.shape[0] // 2, 2) + x.shape[1:])
        x = pairs[:, 0] + swap(pairs[:, 1], axis, bit)
    return x[0]


def part_orders(per):
    bits = bits_of("col")[::-1]
    turned = bits[:-2] + bits[-1:] + bits[-2:-1]
    return [bits, turned] if per % 2 == 0 and len(bits) > 1 else [bits]


def gather_pieces(blocks, beside):
    orders = part_orders(blocks.shape[0])
    size = blocks.shape[0] // len(orders)
    near = [0]
    for bit in orders[0][:-2]:
        near = near + [far | bit for far in near]
    whole = [blocks if far == 0 else swap(blocks, "col", far) for far in near]
    (whole,) = beside(0, [jnp.stack(whole)])
    held = [whole[:, i * size : (i + 1) * size] for i in range(len(orders))]
    if len(orders[0]) > 1:
        came = [swap(x, "col", order[-2]) for x, order in zip(held, orders)]
        held = beside(1, [jnp.concatenate([x, y], axis=0) for x, y in zip(held, came)])
    came = [swap(x, "col", order[-1]) for x, order in zip(held, orders)]
    shape = (-1,) + blocks.shape[1:]
    return [[x.reshape(shape), y.reshape(shape)] for x, y in zip(held, came)]


def piece_index(per, far, block, rho=0, n_row=1):
    orders = part_orders(per)
    size = per // len(orders)
    half = lax.axis_size("col") // 2
    result = 0
    for i, order in enumerate(orders):
        spot = sum(((far & bit) > 0).astype(jnp.int32) << t for t, bit in enumerate(order))
        piece = (i * n_row + rho) * 2 + spot // half
        here = (piece * half + spot % half) * size + block % size
        result = jnp.where(block // size == i, here, result)
    return result


def split_rows(x):
    n, mine = lax.axis_size("row"), lax.axis_index("row")
    size = -(-x.shape[0] // (8 * n)) * 8
    x = jnp.pad(x, ((0, n * size - x.shape[0]), (0, 0)))
    parts = [lax.dynamic_slice_in_dim(x, (mine ^ k) * size, size, 0) for k in range(n)]
    return scatter_sum(jnp.stack(parts), "row")


def join_rows(x):
    n, mine = lax.axis_size("row"), lax.axis_index("row")
    parts = [x]
    for bit in bits_of("row"):
        parts = parts + [swap(part, "row", bit) for part in parts]
    parts = jnp.stack(parts)
    return jnp.concatenate(
        [lax.dynamic_index_in_dim(parts, mine ^ k, 0, keepdims=False) for k in range(n)]
    )


GROUP = 8
TURN = 4 * GROUP
DEPTH = 5
ROOM = 64
SPARE = 8
FIELD = 1 << 16
UNIT = 2.0**-14
COLS = 32


def tile_rows():
    shape = (8, 16, 128)
    rows = 16 * lax.broadcasted_iota(jnp.int32, shape, 0) + lax.broadcasted_iota(jnp.int32, shape, 1)
    return rows.astype(jnp.float32).astype(jnp.bfloat16)


def blocks_of(lines, rows):
    zero = jnp.zeros((), jnp.bfloat16)
    one = jnp.ones((), jnp.bfloat16)
    empty = jnp.zeros((128, 128), jnp.bfloat16)

    def tile(x):
        return jnp.broadcast_to(x.astype(jnp.float32), (16, 128)).astype(jnp.bfloat16)[None]

    def factors(code):
        o = code >> 16
        w = tile((code & (FIELD - 1)).astype(jnp.float32) * UNIT)
        left = jnp.where(rows == tile(o >> 7), w, zero).reshape(128, 128)
        right = jnp.where(rows == tile(o & 127), one, zero).reshape(128, 128)
        return left, right

    blocks = []
    for u in range(0, len(lines), 2):
        (left, right), (left_too, right_too) = factors(lines[u]), factors(lines[u + 1])
        both = lax.dot_general(
            jnp.concatenate([left, left_too], axis=1),
            jnp.concatenate(
                [
                    jnp.concatenate([right, empty], axis=1),
                    jnp.concatenate([empty, right_too], axis=1),
                ],
                axis=0,
            ),
            (((1,), (1,)), ((), ())),
            preferred_element_type=jnp.float32,
        ).astype(jnp.bfloat16)
        blocks += [both[:, :128], both[:, 128:]]
    return blocks


def column(row):
    return jnp.broadcast_to(row, (8, row.shape[1])).T[:, :1]


def ranks(key):
    n = key.shape[1]
    key_column = column(key)
    lanes = lax.broadcasted_iota(jnp.int32, (128, n), 1)
    lines = lax.broadcasted_iota(jnp.int32, (128, n), 0)
    rank = jnp.zeros((1, n), jnp.float32)
    for t in range(0, n, 128):
        before = (key_column[t : t + 128] == key) & (lines + t < lanes)
        rank += jnp.sum(jnp.where(before, 1.0, 0.0), axis=0, keepdims=True)
    return rank


def pack_kernel(per, owners, count, brow, bcol, offs, wts, out, codes, pos_row, pos, sem):
    slots, width = offs.shape
    stride = ROOM + SPARE
    lanes = lax.broadcasted_iota(jnp.int32, (1, slots), 1)
    live = lanes < count[0, 0]
    row = brow[...].astype(jnp.float32)
    home = jnp.floor((row + 0.5) * (1.0 / per))
    key = jnp.where(live, home, float(owners))
    rank = ranks(key)
    fits = live & (rank < ROOM)
    trash = float(ROOM + SPARE - 1)
    pos_row[...] = jnp.where(fits, home * stride + rank, trash).astype(jnp.int32)
    copy = pltpu.make_async_copy(pos_row, pos, sem)
    copy.start()

    out[...] = jnp.zeros_like(out)
    codes[pl.ds(0, slots), :] = offs[...] * FIELD + (
        wts[...].astype(jnp.float32) * (1.0 / UNIT)
    ).astype(jnp.int32)
    codes[pl.ds(slots, 8), :] = jnp.zeros((8, width), jnp.int32)

    label = 1.0 + (row - per * home) * COLS + bcol[...].astype(jnp.float32)
    names = lax.broadcasted_iota(jnp.int32, (owners, slots), 0).astype(jnp.float32)
    chosen = jnp.where((names == key) & fits, label, 0.0).astype(jnp.bfloat16)
    spots = lax.broadcasted_iota(jnp.int32, (1, 128), 1)
    placed = jnp.where(column(rank) == spots.astype(jnp.float32), 1.0, 0.0).astype(jnp.bfloat16)
    labels = jnp.dot(chosen, placed, preferred_element_type=jnp.float32)
    over = jnp.max(jnp.where(live, rank, 0.0), axis=1, keepdims=True)
    labels = jnp.where(spots < ROOM, labels, jnp.where(over < ROOM, 0.0, 1.0)).astype(jnp.int32)
    for k in range(owners):
        out[pl.ds(k * stride + ROOM, 1), :] = labels[k : k + 1]
    copy.wait()

    def turn(i, _):
        for u in range(GROUP):
            s = i * GROUP + u
            out[pl.ds(pos[0, s], 1), :] = codes[pl.ds(s, 1), :]
        return 0

    lax.fori_loop(0, (count[0, 0] + GROUP - 1) // GROUP, turn, 0)


def build_kernel(span, marks, lists, codes, *refs):
    dense, dbuf, sems = refs[-3:]
    start, turns = marks[0, span[0]], marks[0, span[1]]
    rows = tile_rows()

    def out_copy(i):
        slot = lax.rem(i, DEPTH)
        return pltpu.make_async_copy(
            dbuf.at[slot], dense.at[pl.ds(i * TURN, TURN)], sems.at[slot]
        )

    def turn(i, _):
        slot = lax.rem(i, DEPTH)

        @pl.when(i >= start + DEPTH)
        def _():
            out_copy(i - DEPTH).wait()

        lines = [codes[pl.ds(lists[0, i * TURN + u], 1), :] for u in range(TURN)]
        for u in range(0, TURN, GROUP):
            blocks = blocks_of(lines[u : u + GROUP], rows)
            for k, block in enumerate(blocks):
                dbuf[slot, u + k] = block
        out_copy(i).start()
        return 0

    lax.fori_loop(start, turns, turn, 0)

    def finish(i, _):
        out_copy(i).wait()
        return 0

    lax.fori_loop(jnp.maximum(turns - DEPTH, start), turns, finish, 0)


def fetch(pieces, into, sems):
    size = pieces[0].shape[0]
    copies = [
        pltpu.make_async_copy(piece, into.at[pl.ds(i * size, size)], sems.at[i])
        for i, piece in enumerate(pieces)
    ]
    for copy in copies:
        copy.start()
    return copies


def read_dense(start, turns, dense, dbuf, sems, product, prepare):
    def in_copy(i):
        slot = lax.rem(i, DEPTH)
        return pltpu.make_async_copy(
            dense.at[pl.ds(i * TURN, TURN)], dbuf.at[slot], sems.at[slot]
        )

    def begin(i, _):
        in_copy(i).start()
        return 0

    lax.fori_loop(start, jnp.minimum(turns, start + DEPTH - 1), begin, 0)
    prepare()

    def turn(i, _):
        @pl.when(i + DEPTH - 1 < turns)
        def _():
            in_copy(i + DEPTH - 1).start()

        in_copy(i).wait()
        product(i, lax.rem(i, DEPTH))
        return 0

    lax.fori_loop(start, turns, turn, 0)


def add_pairs(i, owner, one, into):
    groups = TURN // GROUP
    for g in range(0, groups, 2):
        added = [one(g), one(g + 1)]
        for k in range(2):
            into[owner[0, i * groups + g + k]] += added[k]


def forward_kernel(n, scale, span, marks, lists, owner, weight, bias, cotangent, dense, *refs):
    pieces, refs = refs[:n], refs[n:]
    output, turned, local, totals, feat, proj, dbuf, piece_sems, sems = refs
    copies = fetch(pieces, feat, piece_sems)
    size, _, width = pieces[0].shape
    batch = 8 if size % 8 == 0 else 1

    def project(t, _):
        spot = pl.ds(t * batch, batch)
        held = feat[spot].reshape(batch * 128, width)
        low = jnp.dot(held, weight[...], preferred_element_type=jnp.float32)
        proj[spot] = low.astype(jnp.bfloat16).reshape(batch, 128, width)
        return 0

    def prepare():
        totals[...] = jnp.zeros_like(totals)
        for i, copy in enumerate(copies):
            copy.wait()
            lax.fori_loop(i * size // batch, (i + 1) * size // batch, project, 0)

    def product(i, slot):
        def one(g):
            spots = [lists[1, i * TURN + g * GROUP + u] for u in range(GROUP)]
            left = jnp.concatenate([dbuf[slot, g * GROUP + u] for u in range(GROUP)], axis=1)
            right = jnp.concatenate(
                [jnp.concatenate([proj[c], feat[c]], axis=1) for c in spots], axis=0
            )
            return jnp.dot(left, right, preferred_element_type=jnp.float32)

        add_pairs(i, owner, one, totals)

    read_dense(marks[0, span[0]], marks[0, span[1]], dense, dbuf, sems, product, prepare)

    weight_sum, bias_sum = 0.0, 0.0
    for q in range(totals.shape[0]):
        lines = pl.ds(q * 128, 128)
        pre = totals[q, :, :width] + bias[...]
        output[lines, :] = jnp.maximum(pre, 0.0).astype(jnp.bfloat16)
        grad = jnp.where(pre > 0, cotangent[lines, :].astype(jnp.float32), 0.0)
        turned[q] = grad.T.astype(jnp.bfloat16)
        weight_sum += lax.dot_general(
            totals[q, :, width:].astype(jnp.bfloat16),
            grad.astype(jnp.bfloat16),
            (((0,), (0,)), ((), ())),
            preferred_element_type=jnp.float32,
        )
        bias_sum += jnp.sum(grad, axis=0, keepdims=True)
    local[pl.ds(0, width), :] = weight_sum * scale
    local[pl.ds(width, 8), :] = jnp.broadcast_to(bias_sum * scale, (8, width))


def tile_kernel(meta, order, dst, col, codes, panel, totals):
    rows = tile_rows()
    totals[...] = jnp.zeros_like(totals)

    def turn(i, _):
        lines = [codes[pl.ds(order[i * GROUP + u], 1), :] for u in range(GROUP)]
        for u, block in enumerate(blocks_of(lines, rows)):
            p = i * GROUP + u
            totals[dst[p]] += jnp.dot(block, panel[col[p]], preferred_element_type=jnp.float32)
        return 0

    lax.fori_loop(0, meta[0], turn, 0)


def backward_kernel(n, span, marks, lists, owner, before, dense, *refs):
    pieces, (acc, grad, dbuf, piece_sems, sems) = refs[:n], refs[n:]
    copies = fetch(pieces, grad, piece_sems)

    def prepare():
        acc[...] = before[...]
        for copy in copies:
            copy.wait()

    def product(i, slot):
        def one(g):
            spots = [lists[1, i * TURN + g * GROUP + u] for u in range(GROUP)]
            left = jnp.concatenate([grad[c] for c in spots], axis=1)
            right = dbuf[slot, pl.ds(g * GROUP, GROUP)].reshape(GROUP * 128, 128)
            return jnp.dot(left, right, preferred_element_type=jnp.float32)

        add_pairs(i, owner, one, acc)

    read_dense(marks[0, span[0]], marks[0, span[1]], dense, dbuf, sems, product, prepare)


SMEM = pl.BlockSpec(memory_space=pltpu.SMEM)
VMEM = pl.BlockSpec(memory_space=pltpu.VMEM)
HBM = pl.BlockSpec(memory_space=pl.ANY)
PARAMS = pltpu.CompilerParams(vmem_limit_bytes=48 * 1024 * 1024)


def cost(slots, products):
    flops = 2 * slots * products * 128**3
    return pl.CostEstimate(flops=flops, bytes_accessed=slots * 128 * 128 * 2, transcendentals=0)


def run_tile(meta, order, dst, col, codes, panel, row_blocks):
    return pl.pallas_call(
        tile_kernel,
        out_shape=jax.ShapeDtypeStruct((row_blocks, 128, panel.shape[-1]), jnp.float32),
        in_specs=[SMEM] * 4 + [VMEM] * 2,
        out_specs=VMEM,
        compiler_params=PARAMS,
    )(meta, order, dst, col, codes, panel)


def run_pack(per, owners, count, brow, bcol, offs, wts):
    slots = brow.shape[1]
    return pl.pallas_call(
        functools.partial(pack_kernel, per, owners),
        out_shape=(
            jax.ShapeDtypeStruct((owners * (ROOM + SPARE), 128), jnp.int32),
            jax.ShapeDtypeStruct((slots + 8, 128), jnp.int32),
        ),
        in_specs=[SMEM] + [VMEM] * 4,
        out_specs=[VMEM] * 2,
        scratch_shapes=[
            pltpu.VMEM((1, slots), jnp.int32),
            pltpu.SMEM((1, slots), jnp.int32),
            pltpu.SemaphoreType.DMA,
        ],
        compiler_params=PARAMS,
    )(count, brow, bcol, offs, wts)


def run_build(span, listed, codes, after, dense):
    lists, _, marks = listed
    others = after if dense is None else after + [dense]
    return pl.pallas_call(
        functools.partial(build_kernel, span),
        out_shape=jax.ShapeDtypeStruct((lists.shape[1], 128, 128), jnp.bfloat16),
        in_specs=[SMEM] * 2 + [VMEM] + [HBM] * len(others),
        out_specs=HBM,
        scratch_shapes=[
            pltpu.VMEM((DEPTH, TURN, 128, 128), jnp.bfloat16),
            pltpu.SemaphoreType.DMA((DEPTH,)),
        ],
        input_output_aliases={} if dense is None else {2 + len(others): 0},
        compiler_params=PARAMS,
        cost_estimate=cost(lists.shape[1], 2),
    )(marks, lists, codes, *others)


def run_forward(scale, span, listed, weight, bias, cotangent, dense, feat):
    lists, owner, marks = listed
    n = len(feat)
    size, _, width = feat[0].shape
    row_blocks = cotangent.shape[0] // 128
    return pl.pallas_call(
        functools.partial(forward_kernel, n, scale, span),
        out_shape=(
            jax.ShapeDtypeStruct(cotangent.shape, jnp.bfloat16),
            jax.ShapeDtypeStruct((row_blocks, width, 128), jnp.bfloat16),
            jax.ShapeDtypeStruct((width + 8, width), jnp.float32),
        ),
        in_specs=[SMEM] * 3 + [VMEM] * 3 + [HBM] * (n + 1),
        out_specs=[VMEM] * 3,
        scratch_shapes=[
            pltpu.VMEM((row_blocks, 128, 2 * width), jnp.float32),
            pltpu.VMEM((n * size, 128, width), jnp.bfloat16),
            pltpu.VMEM((n * size, 128, width), jnp.bfloat16),
            pltpu.VMEM((DEPTH, TURN, 128, 128), jnp.bfloat16),
            pltpu.SemaphoreType.DMA((n,)),
            pltpu.SemaphoreType.DMA((DEPTH,)),
        ],
        compiler_params=PARAMS,
        cost_estimate=cost(lists.shape[1], 4),
    )(marks, lists, owner, weight, bias, cotangent, dense, *feat)


def run_backward(span, listed, before, dense, pieces):
    lists, owner, marks = listed
    n = len(pieces)
    size, width, _ = pieces[0].shape
    return pl.pallas_call(
        functools.partial(backward_kernel, n, span),
        out_shape=jax.ShapeDtypeStruct(before.shape, jnp.float32),
        in_specs=[SMEM] * 3 + [VMEM] + [HBM] * (n + 1),
        out_specs=VMEM,
        scratch_shapes=[
            pltpu.VMEM((n * size, width, 128), jnp.bfloat16),
            pltpu.VMEM((DEPTH, TURN, 128, 128), jnp.bfloat16),
            pltpu.SemaphoreType.DMA((n,)),
            pltpu.SemaphoreType.DMA((DEPTH,)),
        ],
        compiler_params=PARAMS,
        cost_estimate=cost(lists.shape[1], 4),
    )(marks, lists, owner, before, dense, *pieces)


def list_kernel(keys, split, fills, key_ref, *refs):
    value_refs, (lists, owner_ref, marks_ref) = refs[: len(fills)], refs[len(fills) :]
    n, length = key_ref.shape[1], lists.shape[1]
    key = key_ref[...].astype(jnp.float32)
    rank = ranks(key)

    rows = -(-keys // 8) * 8
    names = lax.broadcasted_iota(jnp.int32, (rows, n), 0).astype(jnp.float32)
    name = lax.broadcasted_iota(jnp.int32, (rows, 1), 0).astype(jnp.float32)
    counts = jnp.sum(jnp.where(names == key, 1.0, 0.0), axis=1, keepdims=True)
    filled = jnp.where(name < keys, jnp.floor((counts + (GROUP - 1)) * (1.0 / GROUP)) * GROUP, 0.0)
    below = jnp.sum(jnp.where(name < split, filled, 0.0), axis=0, keepdims=True)
    first = jnp.floor((below + (TURN - 1)) * (1.0 / TURN))
    filled = filled + jnp.where(name == split - 1, first * TURN - below, 0.0)
    turns = jnp.floor((jnp.sum(filled, axis=0, keepdims=True) + (TURN - 1)) * (1.0 / TURN))
    base = jnp.sum(jnp.where(names < key, filled, 0.0), axis=0, keepdims=True)
    pos_column = column(jnp.where(key < keys, base + rank, -1.0))

    spots = lax.broadcasted_iota(jnp.int32, (1, length), 1).astype(jnp.float32)
    columns = [column(ref[...].astype(jnp.float32)) for ref in value_refs]
    sums = [jnp.zeros((1, length), jnp.float32) for _ in fills]
    for t in range(0, n, 128):
        hit = pos_column[t : t + 128] == spots
        for k, fill in enumerate(fills):
            value = columns[k][t : t + 128] - fill
            sums[k] += jnp.sum(jnp.where(hit, value, 0.0), axis=0, keepdims=True)
    for k, fill in enumerate(fills):
        lists[pl.ds(k, 1), :] = (sums[k] + fill).astype(jnp.int32)

    other = lax.broadcasted_iota(jnp.int32, (rows, 128), 1).astype(jnp.float32)
    ends = column(jnp.sum(jnp.where(name <= other, filled, 0.0), axis=0, keepdims=True))[:rows]
    starts = lax.broadcasted_iota(jnp.int32, owner_ref.shape, 1).astype(jnp.float32) * GROUP
    passed = (ends <= starts) & (name < keys)
    owner = jnp.sum(jnp.where(passed, 1.0, 0.0), axis=0, keepdims=True)
    owner = jnp.minimum(owner, keys - 1.0)
    owner_ref[...] = jnp.where(owner >= split, owner - split, owner).astype(jnp.int32)

    spot = lax.broadcasted_iota(jnp.int32, (1, 128), 1)
    marks = jnp.where(spot == FIRST, first, 0.0)
    for k in range(1, 5):
        marks = jnp.where(spot == FIRST + k, jnp.floor(turns * (k / 4)), marks)
    marks_ref[...] = marks.astype(jnp.int32)


FIRST = 1
QUARTERS = [0, 2, 3, 4, 5]


def make_lists(key, values, fills, keys, split):
    n = key.size
    length = (-(-(n + keys * GROUP) // TURN) + 1) * TURN
    groups = -(-length // GROUP // 128) * 128
    lists, owner, marks = pl.pallas_call(
        functools.partial(list_kernel, keys, split, fills),
        out_shape=(
            jax.ShapeDtypeStruct((len(fills), length), jnp.int32),
            jax.ShapeDtypeStruct((1, groups), jnp.int32),
            jax.ShapeDtypeStruct((1, 128), jnp.int32),
        ),
        in_specs=[VMEM] * (1 + len(fills)),
        out_specs=[VMEM] * 3,
        compiler_params=PARAMS,
        cost_estimate=cost(32, 2),
    )(key.reshape(1, n), *[value.reshape(1, n) for value in values])
    return lists, owner, marks


def place(pos, value, length, fill):
    spots = jnp.arange(length, dtype=jnp.int32)
    hit = pos[:, None] == spots[None, :]
    return jnp.sum(jnp.where(hit, value[:, None] - fill, 0), axis=0) + fill


def shards(
    features,
    weight,
    bias,
    cotangent,
    block_count,
    block_rows,
    block_cols,
    edge_offsets,
    edge_weight,
):
    node_dev, width = features.shape
    n_row = lax.axis_size("row")
    n_col = lax.axis_size("col")
    slots = block_rows.shape[2]
    count = block_count[0, 0]
    mine = lax.axis_index("col")
    mine_row = lax.axis_index("row")
    per = node_dev // 128
    row_blocks = per * n_col
    col_blocks = per * n_row
    scale = (node_dev * n_row * n_col) ** (-0.5)
    by_owner = n_row * n_col * node_dev * width * 2 <= 8 * 1024 * 1024
    by_owner = by_owner and col_blocks <= COLS and per * COLS < 256 and n_col % 8 == 0

    brow = block_rows[0, 0]
    bcol = block_cols[0, 0]
    ids = jnp.arange(slots, dtype=jnp.int32)
    live = ids < count
    packed, codes = run_pack(
        per, n_col, block_count, block_rows[0], block_cols[0], edge_offsets[0, 0], edge_weight[0, 0]
    )
    home = brow // per
    turns_plain = ((count + GROUP - 1) // GROUP).reshape(1)

    def tile_plan():
        wide = lax.all_gather(features, "row", axis=0, tiled=True)
        low = jnp.dot(wide, weight, preferred_element_type=jnp.float32).astype(jnp.bfloat16)
        panel = jnp.concatenate([low, wide], axis=1).reshape(col_blocks, 128, 2 * width)
        order = jnp.where(live, ids, slots)
        dst = jnp.where(live, (home ^ mine) * per + brow % per, 0)
        totals = run_tile(turns_plain, order, dst, bcol, codes, panel, row_blocks)
        own = scatter_sum(totals.reshape(n_col, node_dev, 2 * width), "col")
        pre = own[:, :width] + bias
        output = jnp.maximum(pre, 0.0).astype(jnp.bfloat16)
        grad = jnp.where(pre > 0, cotangent.astype(jnp.float32), 0.0)
        turned = jnp.swapaxes(grad.astype(jnp.bfloat16).reshape(per, 128, width), 1, 2)
        weight_sum = lax.dot_general(
            own[:, width:].astype(jnp.bfloat16),
            grad.astype(jnp.bfloat16),
            (((0,), (0,)), ((), ())),
            preferred_element_type=jnp.float32,
        )
        bias_sum = jnp.broadcast_to(jnp.sum(grad, axis=0), (8, width))
        return output, turned, jnp.concatenate([weight_sum, bias_sum], axis=0) * scale

    source = piece_index(per, home ^ mine, brow % per)
    unit = row_blocks // (2 * len(part_orders(per)))
    late = source // unit % 2
    source = source // (2 * unit) * unit + source % unit
    back_key = jnp.where(live, late * col_blocks + bcol, 2 * col_blocks)
    state = {"dense": None}

    def list_backward(key, value):
        return make_lists(key, [ids, value], [slots, 0], 2 * col_blocks, col_blocks)

    def build(held, start, end):
        span = (QUARTERS[start], QUARTERS[end])
        state["dense"] = run_build(span, state["back"], codes, held, state["dense"])

    if by_owner:
        stride = ROOM + SPARE
        came = lax.all_to_all(
            packed.reshape(n_col, stride, 128), "col", split_axis=0, concat_axis=0, tiled=True
        )
        spread = jnp.max(came[:, ROOM, ROOM:], axis=0)[None]
        for bit in bits_of("row"):
            spread = spread + swap(spread, "row", bit)
        any_over = jnp.max(spread, axis=1)

        got = came[:, ROOM, :ROOM]
        sources = jnp.arange(n_col, dtype=jnp.int32)[:, None]
        places = jnp.arange(ROOM, dtype=jnp.int32)[None, :]
        row_here = ((got - 1) // COLS).reshape(-1)
        col_there = (got - 1) % COLS
        col_there = piece_index(
            per, sources ^ mine, col_there % per, (col_there // per) ^ mine_row, n_row
        )
        line = sources * stride + places
        listed = make_lists(
            jnp.where(got > 0, row_here.reshape(got.shape), per),
            [jnp.broadcast_to(line, got.shape), col_there],
            [ROOM + 1, 0],
            per,
            per,
        )

        def prepare(step, held):
            if step == 0:
                held, inputs = lax.optimization_barrier((held, (back_key, source)))
                state["back"] = list_backward(*inputs)
                build(held, 0, 2)
            if step == 1:
                held, state["dense"] = lax.optimization_barrier((held, state["dense"]))
            return held

        pairs = gather_pieces(features.reshape(per, 128, width), prepare)
        lines = came.reshape(n_col * stride, 128)
        here = run_build((0, QUARTERS[4]), listed, lines, [], None)
        last, here = lax.optimization_barrier(([pair[1] for pair in pairs], here))
        feat = []
        for pair in [[pair[0], x] for pair, x in zip(pairs, last)]:
            rows = [pair]
            for bit in bits_of("row"):
                rows = rows + [[swap(x, "row", bit) for x in pair] for pair in rows]
            feat += [x for pair in rows for x in pair]
        done = run_forward(
            scale, (0, QUARTERS[4]), listed, weight, bias[None], cotangent, here, feat
        )
        done = lax.cond(any_over[0] > 0, tile_plan, lambda: tuple(done))
    else:
        state["back"] = list_backward(back_key, source)
        build([features], 0, 2)
        done = tile_plan()

    output, turned, total = done
    turned = with_layout_constraint(turned, Layout(major_to_minor=(0, 1, 2)))
    steps = bits_of("col")

    def add_total():
        state["total"] = state["total"] + swap(state["total"], "col", steps.pop(0))

    def beside(step, held):
        held, state["total"], state["dense"] = lax.optimization_barrier(
            (held, state["total"], state["dense"])
        )
        if steps:
            add_total()
        if step == 1:
            add_products(0, held)
        return held

    def add_products(half, pieces):
        pieces = [x.reshape((-1,) + x.shape[2:]) if x.ndim == 4 else x for x in pieces]
        state["acc"] = run_backward(
            [(0, FIRST), (FIRST, QUARTERS[4])][half], state["back"], state["acc"], state["dense"], pieces
        )

    state["acc"] = jnp.zeros((col_blocks, width, 128), jnp.float32)
    state["total"] = split_rows(total)
    while len(steps) > 3:
        add_total()
    build([turned], 2, 4)
    if len(steps) > 2:
        state["dense"], state["total"] = lax.optimization_barrier(
            (state["dense"], state["total"])
        )
        add_total()
    grad = gather_pieces(turned, beside)
    late_pieces, state["total"] = lax.optimization_barrier(
        ([pair[1] for pair in grad], state["total"])
    )
    while steps:
        add_total()
    total = join_rows(state["total"])
    add_products(1, late_pieces)
    acc = state["acc"]
    back = jnp.swapaxes(acc, 1, 2).reshape(col_blocks * 128, width)
    grad_proj = scatter_sum(
        jnp.stack(
            [
                lax.dynamic_slice_in_dim(back, (mine_row ^ k) * node_dev, node_dev, 0)
                for k in range(n_row)
            ]
        ),
        "row",
    ).astype(jnp.bfloat16)
    grad_features = lax.dot_general(
        grad_proj, weight, (((1,), (1,)), ((), ())), preferred_element_type=jnp.float32
    ).astype(jnp.bfloat16)
    return (
        output,
        grad_features,
        total[: weight.shape[0]],
        total[weight.shape[0]],
    )


def solution(mesh):
    return jax.shard_map(
        shards,
        mesh=mesh,
        in_specs=(
            P(("row", "col"), None),
            P(),
            P(),
            P(("row", "col"), None),
            P("row", "col"),
            P("row", "col", None),
            P("row", "col", None),
            P("row", "col", None, None),
            P("row", "col", None, None),
        ),
        out_specs=(P(("row", "col"), None), P(("row", "col"), None), P(), P()),
        check_vma=False,
    )
```

profile of v0, /device:TPU:9, one launch (start us, length us, event | category | flops | bytes accessed | tf_op | source)
XLA Modules:
  0.0 115.9 jit_solution(510935063154160610)
XLA Ops:
  2.0 2.2 %collective-permute-start.6 = (bf16[4,128,128]{2,1,0:T(8,128)(2,1)}, bf16[4,128,128]{2,1,0:T(8,128)(2,1)S(1)}, u32[]{:S(2)}, u32[]{:S(2)}) collective-permute-start(bf16[4,128,128]{2,1,0:T(8,128)(2,1)} %bitcast.159), channel_id=1, source_target_pairs={{0,4},{1,5},{2,6},{3,7},{4,0},{5,1},{6,2},{7,3},{8,12},{9,13},{10,... | collective-permute-start | bytes 393224 | tf_op jit(solution)/shard_map/ppermute | solution.py:14
  6.7 2.5 %shard_map.120 = (s32[1152,128]{1,0:T(8,128)}, s32[520,128]{1,0:T(8,128)S(1)}) custom-call(s32[1,1]{1,0:T(1,128)} %copy.62.count, s32[1,512]{1,0:T(1,128)} %bitcast.174, s32[1,512]{1,0:T(1,128)} %bitcast.171, s32[512,128]{1,0:T(8,128)S(1)} %bitcast.140, bf16[512,128]{1,0:T(8,128)(2,1)S(1)} %bitcast.141), custom_call_target="tpu_custom_call" | custom-call | tf_op jit(solution)/shard_map/pallas_call | solution.py:381
  9.3 7.3 %all-to-all-start = ((s32[16,72,128]{2,1,0:T(8,128)}), s32[16,72,128]{2,1,0:T(8,128)S(1)}, u32[]{:S(2)}, u32[]{:S(2)}) async-start(s32[16,72,128]{2,1,0:T(8,128)} %bitcast.20), calls=%async_computation | async-start | bytes 1179648 | tf_op jit(solution)/shard_map/all_to_all | solution.py:608
  23.8 3.4 %shard_map.123.refs_1_ = bf16[672,128,128]{2,1,0:T(8,128)(2,1)} custom-call(s32[1,128]{1,0:T(1,128)S(1)} %get-tuple-element.95.marks, s32[2,672]{1,0:T(2,128)S(1)} %get-tuple-element.96.lists, s32[520,128]{1,0:T(8,128)S(1)} %get-tuple-element.97.codes, bf16[4,4,128,128]{3,2,1,0:T(8,128)(2,1)S(1)} %pad_maximum_fusion.1.refs_0_), custom_call_target="tpu_custom_call" | custom-call | flops 5637144576 | bytes 22020096 | tf_op jit(solution)/shard_map/pallas_call | solution.py:401
  27.2 2.6 %collective-permute-done.8 = bf16[4,2,128,128]{3,2,1,0:T(8,128)(2,1)S(1)} collective-permute-done((bf16[4,2,128,128]{3,2,1,0:T(8,128)(2,1)S(1)}, bf16[4,2,128,128]{3,2,1,0:T(8,128)(2,1)S(1)}, u32[]{:S(2)}, u32[]{:S(2)}) %collective-permute-start.8) | collective-permute-done | bytes 262176 | tf_op jit(solution)/shard_map/ppermute | solution.py:14
  29.8 2.2 %collective-permute-done.9 = bf16[4,2,128,128]{3,2,1,0:T(8,128)(2,1)S(1)} collective-permute-done((bf16[4,2,128,128]{3,2,1,0:T(8,128)(2,1)S(1)}, bf16[4,2,128,128]{3,2,1,0:T(8,128)(2,1)S(1)}, u32[]{:S(2)}, u32[]{:S(2)}) %collective-permute-start.9) | collective-permute-done | bytes 262176 | tf_op jit(solution)/shard_map/ppermute | solution.py:14
  32.1 2.3 %collective-permute-start.10 = (bf16[8,2,128,128]{3,2,1,0:T(8,128)(2,1)S(1)}, bf16[8,2,128,128]{3,2,1,0:T(8,128)(2,1)S(1)}, u32[]{:S(2)}, u32[]{:S(2)}) collective-permute-start(bf16[8,2,128,128]{3,2,1,0:T(8,128)(2,1)S(1)} %pad_maximum_fusion.2), channel_id=1, source_target_pairs={{0,1},{1,0},{2,3},{3,2},{4,5},{5,4},{6,7},{7,6},{8,9},{9,8},{10,11... | collective-permute-start | bytes 1572872 | tf_op jit(solution)/shard_map/ppermute | solution.py:14
  34.7 1.7 %collective-permute-start.12 = (bf16[16,128,128]{2,1,0:T(8,128)(2,1)S(1)}, bf16[16,128,128]{2,1,0:T(8,128)(2,1)S(1)}, u32[]{:S(2)}, u32[]{:S(2)}) collective-permute-start(bf16[16,128,128]{2,1,0:T(8,128)(2,1)S(1)} %bitcast.133), channel_id=1, source_target_pairs={{0,16},{16,0},{1,17},{17,1},{2,18},{18,2},{3,19},{19,3},{4,20},{20... | collective-permute-start | bytes 1572872 | tf_op jit(solution)/shard_map/ppermute | solution.py:14
  36.9 2.3 %shard_map.121 = (s32[2,1088]{1,0:T(2,128)S(1)}, s32[1,256]{1,0:T(1,128)S(1)}, s32[1,128]{1,0:T(1,128)S(1)}) custom-call(s32[1,1024]{1,0:T(1,128)S(1)} %get-tuple-element.207.key_ref, s32[1,1024]{1,0:T(1,128)S(1)} %add.440.refs_0_, s32[1,1024]{1,0:T(1,128)S(1)} %get-tuple-element.206.refs_1_), custom_call_target="tpu_custom_call" | custom-call | flops 268435456 | bytes 1048576 | tf_op jit(solution)/shard_map/pallas_call | solution.py:515
  39.2 10.2 %shard_map.124.dense = bf16[1088,128,128]{2,1,0:T(8,128)(2,1)} custom-call(s32[1,128]{1,0:T(1,128)S(1)} %get-tuple-element.89.marks, s32[2,1088]{1,0:T(2,128)S(1)} %get-tuple-element.90.lists, s32[1152,128]{1,0:T(8,128)S(1)} %bitcast.131), custom_call_target="tpu_custom_call" | custom-call | flops 9126805504 | bytes 35651584 | tf_op jit(solution)/shard_map/pallas_call | solution.py:401
  53.5 11.0 %shard_map.125 = (bf16[512,128]{1,0:T(8,128)(2,1)}, bf16[4,128,128]{2,1,0:T(8,128)(2,1)}, f32[136,128]{1,0:T(8,128)S(1)}) custom-call(s32[1,128]{1,0:T(1,128)S(1)} %get-tuple-element.89.marks, s32[2,1088]{1,0:T(2,128)S(1)} %get-tuple-element.90.lists, s32[1,256]{1,0:T(1,128)S(1)} %get-tuple-element.91.owner, bf16[128,128]{1,0:T(8,128)(2,1)S(1)} %copy-done.4, ...), custom_call_target="tpu_custom_call" | custom-call | flops 18253611008 | bytes 35651584 | tf_op jit(solution)/shard_map/pallas_call | solution.py:421
  64.8 1.8 %collective-permute-start.18 = (bf16[4,128,128]{2,1,0:T(8,128)(2,1)}, bf16[4,128,128]{2,1,0:T(8,128)(2,1)S(1)}, u32[]{:S(2)}, u32[]{:S(2)}) collective-permute-start(bf16[4,128,128]{2,1,0:T(8,128)(2,1)} %get-tuple-element.186.refs_0_), channel_id=1, source_target_pairs={{0,12},{1,13},{2,14},{3,15},{4,8},{5,9},{6,10},{7,11},{8,4},{9,5},... | collective-permute-start | bytes 393224 | tf_op jit(solution)/shard_map/ppermute | solution.py:14
  68.7 3.4 %shard_map.126.dense = bf16[672,128,128]{2,1,0:T(8,128)(2,1)} custom-call(s32[1,128]{1,0:T(1,128)S(1)} %get-tuple-element.95.marks, s32[2,672]{1,0:T(2,128)S(1)} %get-tuple-element.96.lists, s32[520,128]{1,0:T(8,128)S(1)} %get-tuple-element.97.codes, bf16[4,128,128]{2,1,0:T(8,128)(2,1)} %get-tuple-element.186.refs_0_, ...), custom_call_target="tpu_custom_call", output_to_operand_aliasing={{}: (4, {})} | custom-call | flops 5637144576 | bytes 22020096 | tf_op jit(solution)/shard_map/pallas_call | solution.py:401
  72.1 4.8 %collective-permute-start.21 = (f32[72,128]{1,0:T(8,128)S(1)}, f32[72,128]{1,0:T(8,128)S(1)}, u32[]{:S(2)}, u32[]{:S(2)}) collective-permute-start(f32[72,128]{1,0:T(8,128)S(1)} %add.487), channel_id=1, source_target_pairs={{0,2},{1,3},{2,0},{3,1},{4,6},{5,7},{6,4},{7,5},{8,10},{9,11},{10,... | collective-permute-start | bytes 110600 | tf_op jit(solution)/shard_map/ppermute | solution.py:14
  79.3 1.5 %collective-permute-start.22 = (bf16[4,2,128,128]{3,2,1,0:T(8,128)(2,1)S(1)}, bf16[4,2,128,128]{3,2,1,0:T(8,128)(2,1)S(1)}, u32[]{:S(2)}, u32[]{:S(2)}) collective-permute-start(bf16[4,2,128,128]{3,2,1,0:T(8,128)(2,1)S(1)} %get-tuple-element.199), channel_id=1, source_target_pairs={{0,2},{1,3},{2,0},{3,1},{4,6},{5,7},{6,4},{7,5},{8,10},{9,11},{10,... | collective-permute-start | bytes 786440 | tf_op jit(solution)/shard_map/ppermute | solution.py:14
  80.8 3.9 %collective-permute-start.23 = (bf16[4,2,128,128]{3,2,1,0:T(8,128)(2,1)S(1)}, bf16[4,2,128,128]{3,2,1,0:T(8,128)(2,1)S(1)}, u32[]{:S(2)}, u32[]{:S(2)}) collective-permute-start(bf16[4,2,128,128]{3,2,1,0:T(8,128)(2,1)S(1)} %get-tuple-element.198), channel_id=1, source_target_pairs={{0,1},{1,0},{2,3},{3,2},{4,5},{5,4},{6,7},{7,6},{8,9},{9,8},{10,11... | collective-permute-start | bytes 786440 | tf_op jit(solution)/shard_map/ppermute | solution.py:14
  84.8 2.8 %collective-permute-done.24 = f32[72,128]{1,0:T(8,128)S(1)} collective-permute-done((f32[72,128]{1,0:T(8,128)S(1)}, f32[72,128]{1,0:T(8,128)S(1)}, u32[]{:S(2)}, u32[]{:S(2)}) %collective-permute-start.24) | collective-permute-done | bytes 36896 | tf_op jit(solution)/shard_map/ppermute | solution.py:14
  87.6 2.1 %collective-permute-done.23 = bf16[4,2,128,128]{3,2,1,0:T(8,128)(2,1)S(1)} collective-permute-done((bf16[4,2,128,128]{3,2,1,0:T(8,128)(2,1)S(1)}, bf16[4,2,128,128]{3,2,1,0:T(8,128)(2,1)S(1)}, u32[]{:S(2)}, u32[]{:S(2)}) %collective-permute-start.23) | collective-permute-done | bytes 262176 | tf_op jit(solution)/shard_map/ppermute | solution.py:14
  89.8 2.3 %collective-permute-start.25 = (bf16[8,2,128,128]{3,2,1,0:T(8,128)(2,1)S(1)}, bf16[8,2,128,128]{3,2,1,0:T(8,128)(2,1)S(1)}, u32[]{:S(2)}, u32[]{:S(2)}) collective-permute-start(bf16[8,2,128,128]{3,2,1,0:T(8,128)(2,1)S(1)} %pad_maximum_fusion.5), channel_id=1, source_target_pairs={{0,1},{1,0},{2,3},{3,2},{4,5},{5,4},{6,7},{7,6},{8,9},{9,8},{10,11... | collective-permute-start | bytes 1572872 | tf_op jit(solution)/shard_map/ppermute | solution.py:14
  92.0 2.4 %collective-permute-start.27 = (f32[72,128]{1,0:T(8,128)S(1)}, f32[72,128]{1,0:T(8,128)S(1)}, u32[]{:S(2)}, u32[]{:S(2)}) collective-permute-start(f32[72,128]{1,0:T(8,128)S(1)} %add.489), channel_id=1, source_target_pairs={{0,8},{1,9},{2,10},{3,11},{4,12},{5,13},{6,14},{7,15},{8,0},{9,1},... | collective-permute-start | bytes 110600 | tf_op jit(solution)/shard_map/ppermute | solution.py:14
  94.5 2.9 %shard_map.127.before = f32[8,128,128]{2,1,0:T(8,128)S(1)} custom-call(s32[1,128]{1,0:T(1,128)S(1)} %get-tuple-element.95.marks, s32[2,672]{1,0:T(2,128)S(1)} %get-tuple-element.96.lists, s32[1,128]{1,0:T(1,128)S(1)} %get-tuple-element.107.owner, f32[8,128,128]{2,1,0:T(8,128)S(1)} %broadcast_in_dim.32.before, bf16[672,128,128]{2,1,0:T(8,128)(2,1)} %shard_map.126.dense, ...), custom_call_target="tpu_custom_call" | custom-call | flops 11274289152 | bytes 22020096 | tf_op jit(solution)/shard_map/pallas_call | solution.py:447
  97.4 5.0 %collective-permute-done.25 = bf16[8,2,128,128]{3,2,1,0:T(8,128)(2,1)S(1)} collective-permute-done((bf16[8,2,128,128]{3,2,1,0:T(8,128)(2,1)S(1)}, bf16[8,2,128,128]{3,2,1,0:T(8,128)(2,1)S(1)}, u32[]{:S(2)}, u32[]{:S(2)}) %collective-permute-start.25) | collective-permute-done | bytes 524320 | tf_op jit(solution)/shard_map/ppermute | solution.py:14
  103.6 2.9 %shard_map.128 = f32[8,128,128]{2,1,0:T(8,128)S(1)} custom-call(s32[1,128]{1,0:T(1,128)S(1)} %get-tuple-element.95.marks, s32[2,672]{1,0:T(2,128)S(1)} %get-tuple-element.96.lists, s32[1,128]{1,0:T(1,128)S(1)} %get-tuple-element.107.owner, f32[8,128,128]{2,1,0:T(8,128)S(1)} %shard_map.127.before, bf16[672,128,128]{2,1,0:T(8,128)(2,1)} %shard_map.126.dense, ...), custom_call_target="tpu_custom_call" | custom-call | flops 11274289152 | bytes 22020096 | tf_op jit(solution)/shard_map/pallas_call | solution.py:447
  106.7 6.3 %collective-permute-start.29 = (f32[72,128]{1,0:T(8,128)S(1)}, f32[72,128]{1,0:T(8,128)S(1)}, u32[]{:S(2)}, u32[]{:S(2)}) collective-permute-start(f32[72,128]{1,0:T(8,128)S(1)} %add.490), channel_id=1, source_target_pairs={{0,16},{16,0},{1,17},{17,1},{2,18},{18,2},{3,19},{19,3},{4,20},{20... | collective-permute-start | bytes 110600 | tf_op jit(solution)/shard_map/ppermute | solution.py:14
  (99 shorter events, 24.0 us)
Async XLA Ops:
  0.6 18.7 %collective-permute-start.7 = (bf16[4,128,128]{2,1,0:T(8,128)(2,1)}, bf16[4,128,128]{2,1,0:T(8,128)(2,1)S(1)}, u32[]{:S(2)}, u32[]{:S(2)}) collective-permute-start(bf16[4,128,128]{2,1,0:T(8,128)(2,1)} %bitcast.158), channel_id=1, source_target_pairs={{0,12},{1,13},{2,14},{3,15},{4,8},{5,9},{6,10},{7,11},{8,4},{9,5},... | collective-permute-start | bytes 393224 | tf_op jit(solution)/shard_map/ppermute | solution.py:14
  2.0 17.3 %collective-permute-start.6 = (bf16[4,128,128]{2,1,0:T(8,128)(2,1)}, bf16[4,128,128]{2,1,0:T(8,128)(2,1)S(1)}, u32[]{:S(2)}, u32[]{:S(2)}) collective-permute-start(bf16[4,128,128]{2,1,0:T(8,128)(2,1)} %bitcast.159), channel_id=1, source_target_pairs={{0,4},{1,5},{2,6},{3,7},{4,0},{5,1},{6,2},{7,3},{8,12},{9,13},{10,... | collective-permute-start | bytes 393224 | tf_op jit(solution)/shard_map/ppermute | solution.py:14
  4.2 15.2 %collective-permute-start.5 = (bf16[4,128,128]{2,1,0:T(8,128)(2,1)}, bf16[4,128,128]{2,1,0:T(8,128)(2,1)S(1)}, u32[]{:S(2)}, u32[]{:S(2)}) collective-permute-start(bf16[4,128,128]{2,1,0:T(8,128)(2,1)} %bitcast.160), channel_id=1, source_target_pairs={{0,8},{1,9},{2,10},{3,11},{4,12},{5,13},{6,14},{7,15},{8,0},{9,1},... | collective-permute-start | bytes 393224 | tf_op jit(solution)/shard_map/ppermute | solution.py:14
  9.3 27.2 %all-to-all-start = ((s32[16,72,128]{2,1,0:T(8,128)}), s32[16,72,128]{2,1,0:T(8,128)S(1)}, u32[]{:S(2)}, u32[]{:S(2)}) async-start(s32[16,72,128]{2,1,0:T(8,128)} %bitcast.20), calls=%async_computation | async-start | bytes 1179648 | tf_op jit(solution)/shard_map/all_to_all | solution.py:608
  20.4 9.4 %collective-permute-start.8 = (bf16[4,2,128,128]{3,2,1,0:T(8,128)(2,1)S(1)}, bf16[4,2,128,128]{3,2,1,0:T(8,128)(2,1)S(1)}, u32[]{:S(2)}, u32[]{:S(2)}) collective-permute-start(bf16[4,2,128,128]{3,2,1,0:T(8,128)(2,1)S(1)} %get-tuple-element.201), channel_id=1, source_target_pairs={{0,2},{1,3},{2,0},{3,1},{4,6},{5,7},{6,4},{7,5},{8,10},{9,11},{10,... | collective-permute-start | bytes 786440 | tf_op jit(solution)/shard_map/ppermute | solution.py:14
  21.6 10.4 %collective-permute-start.9 = (bf16[4,2,128,128]{3,2,1,0:T(8,128)(2,1)S(1)}, bf16[4,2,128,128]{3,2,1,0:T(8,128)(2,1)S(1)}, u32[]{:S(2)}, u32[]{:S(2)}) collective-permute-start(bf16[4,2,128,128]{3,2,1,0:T(8,128)(2,1)S(1)} %get-tuple-element.200), channel_id=1, source_target_pairs={{0,1},{1,0},{2,3},{3,2},{4,5},{5,4},{6,7},{7,6},{8,9},{9,8},{10,11... | collective-permute-start | bytes 786440 | tf_op jit(solution)/shard_map/ppermute | solution.py:14
  32.1 17.3 %collective-permute-start.10 = (bf16[8,2,128,128]{3,2,1,0:T(8,128)(2,1)S(1)}, bf16[8,2,128,128]{3,2,1,0:T(8,128)(2,1)S(1)}, u32[]{:S(2)}, u32[]{:S(2)}) collective-permute-start(bf16[8,2,128,128]{3,2,1,0:T(8,128)(2,1)S(1)} %pad_maximum_fusion.2), channel_id=1, source_target_pairs={{0,1},{1,0},{2,3},{3,2},{4,5},{5,4},{6,7},{7,6},{8,9},{9,8},{10,11... | collective-permute-start | bytes 1572872 | tf_op jit(solution)/shard_map/ppermute | solution.py:14
  34.3 15.1 %collective-permute-start.11 = (bf16[8,2,128,128]{3,2,1,0:T(8,128)(2,1)S(1)}, bf16[8,2,128,128]{3,2,1,0:T(8,128)(2,1)S(1)}, u32[]{:S(2)}, u32[]{:S(2)}) collective-permute-start(bf16[8,2,128,128]{3,2,1,0:T(8,128)(2,1)S(1)} %pad_maximum_fusion.3), channel_id=1, source_target_pairs={{0,2},{1,3},{2,0},{3,1},{4,6},{5,7},{6,4},{7,5},{8,10},{9,11},{10,... | collective-permute-start | bytes 1572872 | tf_op jit(solution)/shard_map/ppermute | solution.py:14
  34.7 18.6 %collective-permute-start.12 = (bf16[16,128,128]{2,1,0:T(8,128)(2,1)S(1)}, bf16[16,128,128]{2,1,0:T(8,128)(2,1)S(1)}, u32[]{:S(2)}, u32[]{:S(2)}) collective-permute-start(bf16[16,128,128]{2,1,0:T(8,128)(2,1)S(1)} %bitcast.133), channel_id=1, source_target_pairs={{0,16},{16,0},{1,17},{17,1},{2,18},{18,2},{3,19},{19,3},{4,20},{20... | collective-permute-start | bytes 1572872 | tf_op jit(solution)/shard_map/ppermute | solution.py:14
  36.4 16.9 %collective-permute-start.14 = (bf16[16,128,128]{2,1,0:T(8,128)(2,1)S(1)}, bf16[16,128,128]{2,1,0:T(8,128)(2,1)}, u32[]{:S(2)}, u32[]{:S(2)}) collective-permute-start(bf16[16,128,128]{2,1,0:T(8,128)(2,1)S(1)} %bitcast.135), channel_id=1, source_target_pairs={{0,16},{16,0},{1,17},{17,1},{2,18},{18,2},{3,19},{19,3},{4,20},{20... | collective-permute-start | bytes 1572872 | tf_op jit(solution)/shard_map/ppermute | solution.py:14
  49.4 4.0 %collective-permute-start.13 = (bf16[16,128,128]{2,1,0:T(8,128)(2,1)S(1)}, bf16[16,128,128]{2,1,0:T(8,128)(2,1)S(1)}, u32[]{:S(2)}, u32[]{:S(2)}) collective-permute-start(bf16[16,128,128]{2,1,0:T(8,128)(2,1)S(1)} %bitcast.144), channel_id=1, source_target_pairs={{0,16},{16,0},{1,17},{17,1},{2,18},{18,2},{3,19},{19,3},{4,20},{20... | collective-permute-start | bytes 1572872 | tf_op jit(solution)/shard_map/ppermute | solution.py:14
  49.5 3.9 %collective-permute-start.15 = (bf16[16,128,128]{2,1,0:T(8,128)(2,1)S(1)}, bf16[16,128,128]{2,1,0:T(8,128)(2,1)}, u32[]{:S(2)}, u32[]{:S(2)}) collective-permute-start(bf16[16,128,128]{2,1,0:T(8,128)(2,1)S(1)} %bitcast.146), channel_id=1, source_target_pairs={{0,16},{16,0},{1,17},{17,1},{2,18},{18,2},{3,19},{19,3},{4,20},{20... | collective-permute-start | bytes 1572872 | tf_op jit(solution)/shard_map/ppermute | solution.py:14
  64.7 3.1 %collective-permute-start.19 = (f32[1,72,128]{2,1,0:T(8,128)S(1)}, f32[1,72,128]{2,1,0:T(8,128)S(1)}, u32[]{:S(2)}, u32[]{:S(2)}) collective-permute-start(f32[1,72,128]{2,1,0:T(8,128)S(1)} %slice_bitcast_fusion.10), channel_id=1, source_target_pairs={{0,16},{16,0},{1,17},{17,1},{2,18},{18,2},{3,19},{19,3},{4,20},{20... | collective-permute-start | bytes 110600 | tf_op jit(solution)/shard_map/ppermute | solution.py:14
  64.8 13.5 %collective-permute-start.18 = (bf16[4,128,128]{2,1,0:T(8,128)(2,1)}, bf16[4,128,128]{2,1,0:T(8,128)(2,1)S(1)}, u32[]{:S(2)}, u32[]{:S(2)}) collective-permute-start(bf16[4,128,128]{2,1,0:T(8,128)(2,1)} %get-tuple-element.186.refs_0_), channel_id=1, source_target_pairs={{0,12},{1,13},{2,14},{3,15},{4,8},{5,9},{6,10},{7,11},{8,4},{9,5},... | collective-permute-start | bytes 393224 | tf_op jit(solution)/shard_map/ppermute | solution.py:14
  66.6 11.6 %collective-permute-start.17 = (bf16[4,128,128]{2,1,0:T(8,128)(2,1)}, bf16[4,128,128]{2,1,0:T(8,128)(2,1)S(1)}, u32[]{:S(2)}, u32[]{:S(2)}) collective-permute-start(bf16[4,128,128]{2,1,0:T(8,128)(2,1)} %get-tuple-element.186.refs_0_), channel_id=1, source_target_pairs={{0,4},{1,5},{2,6},{3,7},{4,0},{5,1},{6,2},{7,3},{8,12},{9,13},{10,... | collective-permute-start | bytes 393224 | tf_op jit(solution)/shard_map/ppermute | solution.py:14
  67.8 10.5 %collective-permute-start.16 = (bf16[4,128,128]{2,1,0:T(8,128)(2,1)}, bf16[4,128,128]{2,1,0:T(8,128)(2,1)S(1)}, u32[]{:S(2)}, u32[]{:S(2)}) collective-permute-start(bf16[4,128,128]{2,1,0:T(8,128)(2,1)} %get-tuple-element.186.refs_0_), channel_id=1, source_target_pairs={{0,8},{1,9},{2,10},{3,11},{4,12},{5,13},{6,14},{7,15},{8,0},{9,1},... | collective-permute-start | bytes 393224 | tf_op jit(solution)/shard_map/ppermute | solution.py:14
  67.8 4.3 %collective-permute-start.20 = (f32[72,128]{1,0:T(8,128)S(1)}, f32[72,128]{1,0:T(8,128)S(1)}, u32[]{:S(2)}, u32[]{:S(2)}) collective-permute-start(f32[72,128]{1,0:T(8,128)S(1)} %fusion.23), channel_id=1, source_target_pairs={{0,1},{1,0},{2,3},{3,2},{4,5},{5,4},{6,7},{7,6},{8,9},{9,8},{10,11... | collective-permute-start | bytes 110600 | tf_op jit(solution)/shard_map/ppermute | solution.py:14
  72.1 6.1 %collective-permute-start.21 = (f32[72,128]{1,0:T(8,128)S(1)}, f32[72,128]{1,0:T(8,128)S(1)}, u32[]{:S(2)}, u32[]{:S(2)}) collective-permute-start(f32[72,128]{1,0:T(8,128)S(1)} %add.487), channel_id=1, source_target_pairs={{0,2},{1,3},{2,0},{3,1},{4,6},{5,7},{6,4},{7,5},{8,10},{9,11},{10,... | collective-permute-start | bytes 110600 | tf_op jit(solution)/shard_map/ppermute | solution.py:14
  79.3 8.3 %collective-permute-start.22 = (bf16[4,2,128,128]{3,2,1,0:T(8,128)(2,1)S(1)}, bf16[4,2,128,128]{3,2,1,0:T(8,128)(2,1)S(1)}, u32[]{:S(2)}, u32[]{:S(2)}) collective-permute-start(bf16[4,2,128,128]{3,2,1,0:T(8,128)(2,1)S(1)} %get-tuple-element.199), channel_id=1, source_target_pairs={{0,2},{1,3},{2,0},{3,1},{4,6},{5,7},{6,4},{7,5},{8,10},{9,11},{10,... | collective-permute-start | bytes 786440 | tf_op jit(solution)/shard_map/ppermute | solution.py:14
  80.8 8.9 %collective-permute-start.23 = (bf16[4,2,128,128]{3,2,1,0:T(8,128)(2,1)S(1)}, bf16[4,2,128,128]{3,2,1,0:T(8,128)(2,1)S(1)}, u32[]{:S(2)}, u32[]{:S(2)}) collective-permute-start(bf16[4,2,128,128]{3,2,1,0:T(8,128)(2,1)S(1)} %get-tuple-element.198), channel_id=1, source_target_pairs={{0,1},{1,0},{2,3},{3,2},{4,5},{5,4},{6,7},{7,6},{8,9},{9,8},{10,11... | collective-permute-start | bytes 786440 | tf_op jit(solution)/shard_map/ppermute | solution.py:14
  89.8 12.6 %collective-permute-start.25 = (bf16[8,2,128,128]{3,2,1,0:T(8,128)(2,1)S(1)}, bf16[8,2,128,128]{3,2,1,0:T(8,128)(2,1)S(1)}, u32[]{:S(2)}, u32[]{:S(2)}) collective-permute-start(bf16[8,2,128,128]{3,2,1,0:T(8,128)(2,1)S(1)} %pad_maximum_fusion.5), channel_id=1, source_target_pairs={{0,1},{1,0},{2,3},{3,2},{4,5},{5,4},{6,7},{7,6},{8,9},{9,8},{10,11... | collective-permute-start | bytes 1572872 | tf_op jit(solution)/shard_map/ppermute | solution.py:14
  92.0 11.6 %collective-permute-start.26 = (bf16[8,2,128,128]{3,2,1,0:T(8,128)(2,1)S(1)}, bf16[8,2,128,128]{3,2,1,0:T(8,128)(2,1)S(1)}, u32[]{:S(2)}, u32[]{:S(2)}) collective-permute-start(bf16[8,2,128,128]{3,2,1,0:T(8,128)(2,1)S(1)} %pad_maximum_fusion.6), channel_id=1, source_target_pairs={{0,2},{1,3},{2,0},{3,1},{4,6},{5,7},{6,4},{7,5},{8,10},{9,11},{10,... | collective-permute-start | bytes 1572872 | tf_op jit(solution)/shard_map/ppermute | solution.py:14
  92.0 5.3 %collective-permute-start.27 = (f32[72,128]{1,0:T(8,128)S(1)}, f32[72,128]{1,0:T(8,128)S(1)}, u32[]{:S(2)}, u32[]{:S(2)}) collective-permute-start(f32[72,128]{1,0:T(8,128)S(1)} %add.489), channel_id=1, source_target_pairs={{0,8},{1,9},{2,10},{3,11},{4,12},{5,13},{6,14},{7,15},{8,0},{9,1},... | collective-permute-start | bytes 110600 | tf_op jit(solution)/shard_map/ppermute | solution.py:14
  106.7 7.1 %collective-permute-start.29 = (f32[72,128]{1,0:T(8,128)S(1)}, f32[72,128]{1,0:T(8,128)S(1)}, u32[]{:S(2)}, u32[]{:S(2)}) collective-permute-start(f32[72,128]{1,0:T(8,128)S(1)} %add.490), channel_id=1, source_target_pairs={{0,16},{16,0},{1,17},{17,1},{2,18},{18,2},{3,19},{19,3},{4,20},{20... | collective-permute-start | bytes 110600 | tf_op jit(solution)/shard_map/ppermute | solution.py:14
  (8 other events, 44.4 us)
where the time goes:
time: 114 us; the launch traced here: 116 us
  starting transfers between devices  43.6 us (38%)
  Pallas kernels  39.5 us (35%)
  waiting for transfers between devices  18.9 us (17%)
  other arithmetic  6.37 us (6%)
  local copies, waits for them, and re-layouts  4.19 us (4%)
  between operations  2.35 us (2%)
    ppermute x26, starting transfers between devices, swap(): return lax.ppermute(x, axis, [(i, i ^ bit) for i in range(n)])  36.3 us
    ppermute x26, waiting for transfers between devices, swap(): return lax.ppermute(x, axis, [(i, i ^ bit) for i in range(n)])  18.9 us
    pallas_call x3, Pallas kernels, run_build(): pl.pallas_call(functools.partial(build_kernel, span), out_shape=jax.Shape...  16.9 us
    pallas_call x1, Pallas kernels, run_forward(): pl.pallas_call(functools.partial(forward_kernel, n, scale, span), out_sha...  11 us
    all_to_all x1, starting transfers between devices, shards(): lax.all_to_all(packed.reshape(n_col, stride, 128), 'col', split_axis=0, c...  7.29 us
    pallas_call x2, Pallas kernels, run_backward(): pl.pallas_call(functools.partial(backward_kernel, n, span), out_shape=jax...  5.76 us
    pallas_call x2, Pallas kernels, make_lists(): pl.pallas_call(functools.partial(list_kernel, keys, split, fills), out_sh...  3.3 us
    pallas_call x1, Pallas kernels, run_pack(): pl.pallas_call(functools.partial(pack_kernel, per, owners), out_shape=(ja...  2.54 us
  transfers between devices with their start and end apart: 27, of which 9 were waited for; matrix products, arithmetic and copies ran while one was open for 6% of the time, Pallas kernels for 22%

commit v1 on v0

--- a/solution.py
+++ b/solution.py
@@ -147,8 +147,16 @@
     return rank
 
 
-def pack_kernel(per, owners, count, brow, bcol, offs, wts, out, codes, pos_row, pos, sem):
+def pack_kernel(
+    per, owners, count, brow, bcol, offs_in, wts_in, out, codes, offs, wts, pos_row, pos, sems
+):
     slots, width = offs.shape
+    reads = [
+        pltpu.make_async_copy(offs_in, offs, sems.at[0]),
+        pltpu.make_async_copy(wts_in, wts, sems.at[1]),
+    ]
+    for read in reads:
+        read.start()
     stride = ROOM + SPARE
     lanes = lax.broadcasted_iota(jnp.int32, (1, slots), 1)
     live = lanes < count[0, 0]
@@ -159,15 +167,10 @@
     fits = live & (rank < ROOM)
     trash = float(ROOM + SPARE - 1)
     pos_row[...] = jnp.where(fits, home * stride + rank, trash).astype(jnp.int32)
-    copy = pltpu.make_async_copy(pos_row, pos, sem)
+    copy = pltpu.make_async_copy(pos_row, pos, sems.at[2])
     copy.start()
 
     out[...] = jnp.zeros_like(out)
-    codes[pl.ds(0, slots), :] = offs[...] * FIELD + (
-        wts[...].astype(jnp.float32) * (1.0 / UNIT)
-    ).astype(jnp.int32)
-    codes[pl.ds(slots, 8), :] = jnp.zeros((8, width), jnp.int32)
-
     label = 1.0 + (row - per * home) * COLS + bcol[...].astype(jnp.float32)
     names = lax.broadcasted_iota(jnp.int32, (owners, slots), 0).astype(jnp.float32)
     chosen = jnp.where((names == key) & fits, label, 0.0).astype(jnp.bfloat16)
@@ -178,6 +181,12 @@
     labels = jnp.where(spots < ROOM, labels, jnp.where(over < ROOM, 0.0, 1.0)).astype(jnp.int32)
     for k in range(owners):
         out[pl.ds(k * stride + ROOM, 1), :] = labels[k : k + 1]
+    for read in reads:
+        read.wait()
+    codes[pl.ds(0, slots), :] = offs[...] * FIELD + (
+        wts[...].astype(jnp.float32) * (1.0 / UNIT)
+    ).astype(jnp.int32)
+    codes[pl.ds(slots, 8), :] = jnp.zeros((8, width), jnp.int32)
     copy.wait()
 
     def turn(i, _):
@@ -384,12 +393,14 @@
             jax.ShapeDtypeStruct((owners * (ROOM + SPARE), 128), jnp.int32),
             jax.ShapeDtypeStruct((slots + 8, 128), jnp.int32),
         ),
-        in_specs=[SMEM] + [VMEM] * 4,
+        in_specs=[SMEM] + [VMEM] * 2 + [HBM] * 2,
         out_specs=[VMEM] * 2,
         scratch_shapes=[
+            pltpu.VMEM(offs.shape, offs.dtype),
+            pltpu.VMEM(wts.shape, wts.dtype),
             pltpu.VMEM((1, slots), jnp.int32),
             pltpu.SMEM((1, slots), jnp.int32),
-            pltpu.SemaphoreType.DMA,
+            pltpu.SemaphoreType.DMA((3,)),
         ],
         compiler_params=PARAMS,
     )(count, brow, bcol, offs, wts)
@@ -558,17 +569,16 @@
     by_owner = n_row * n_col * node_dev * width * 2 <= 8 * 1024 * 1024
     by_owner = by_owner and col_blocks <= COLS and per * COLS < 256 and n_col % 8 == 0
 
-    brow = block_rows[0, 0]
-    bcol = block_cols[0, 0]
-    ids = jnp.arange(slots, dtype=jnp.int32)
-    live = ids < count
     packed, codes = run_pack(
         per, n_col, block_count, block_rows[0], block_cols[0], edge_offsets[0, 0], edge_weight[0, 0]
     )
-    home = brow // per
-    turns_plain = ((count + GROUP - 1) // GROUP).reshape(1)
 
     def tile_plan():
+        ids = jnp.arange(slots, dtype=jnp.int32)
+        live = ids < count
+        brow, bcol = block_rows[0, 0], block_cols[0, 0]
+        home = brow // per
+        turns_plain = ((count + GROUP - 1) // GROUP).reshape(1)
         wide = lax.all_gather(features, "row", axis=0, tiled=True)
         low = jnp.dot(wide, weight, preferred_element_type=jnp.float32).astype(jnp.bfloat16)
         panel = jnp.concatenate([low, wide], axis=1).reshape(col_blocks, 128, 2 * width)
@@ -589,15 +599,18 @@
         bias_sum = jnp.broadcast_to(jnp.sum(grad, axis=0), (8, width))
         return output, turned, jnp.concatenate([weight_sum, bias_sum], axis=0) * scale
 
-    source = piece_index(per, home ^ mine, brow % per)
-    unit = row_blocks // (2 * len(part_orders(per)))
-    late = source // unit % 2
-    source = source // (2 * unit) * unit + source % unit
-    back_key = jnp.where(live, late * col_blocks + bcol, 2 * col_blocks)
     state = {"dense": None}
 
-    def list_backward(key, value):
-        return make_lists(key, [ids, value], [slots, 0], 2 * col_blocks, col_blocks)
+    def list_backward(count, brow, bcol):
+        ids = jnp.arange(slots, dtype=jnp.int32)
+        source = piece_index(per, (brow // per) ^ mine, brow % per)
+        unit = row_blocks // (2 * len(part_orders(per)))
+        late = source // unit % 2
+        source = source // (2 * unit) * unit + source % unit
+        key = jnp.where(ids < count, late * col_blocks + bcol, 2 * col_blocks)
+        return make_lists(key, [ids, source], [slots, 0], 2 * col_blocks, col_blocks)
+
+    slot_inputs = (count, block_rows[0, 0], block_cols[0, 0])
 
     def build(held, start, end):
         span = (QUARTERS[start], QUARTERS[end])
@@ -632,7 +645,7 @@
 
         def prepare(step, held):
             if step == 0:
-                held, inputs = lax.optimization_barrier((held, (back_key, source)))
+                held, inputs = lax.optimization_barrier((held, slot_inputs))
                 state["back"] = list_backward(*inputs)
                 build(held, 0, 2)
             if step == 1:
@@ -654,7 +667,7 @@
         )
         done = lax.cond(any_over[0] > 0, tile_plan, lambda: tuple(done))
     else:
-        state["back"] = list_backward(back_key, source)
+        state["back"] = list_backward(*slot_inputs)
         build([features], 0, 2)
         done = tile_plan()
 

time: 114 us -> 113 us (level); the launches traced: 116 us -> 113 us
  starting transfers between devices: 43.6 us -> 25.9 us
  Pallas kernels: 39.5 us -> 56.7 us
    ppermute x26, starting transfers between devices: 36.3 us -> 18.7 us  [swap(): return lax.ppermute(x, axis, [(i, i ^ bit) for i in range(n)])]
    pallas_call x3, Pallas kernels: 16.9 us -> 27.9 us  [run_build(): pl.pallas_call(functools.partial(build_kernel, span), out_shape=jax.Shape...]
    pallas_call x2, Pallas kernels: 5.76 us -> 11.8 us  [run_backward(): pl.pallas_call(functools.partial(backward_kernel, n, span), out_shape=jax...]
  transfers between devices with their start and end apart: 27 -> 27, of which waited for: 9 -> 6; matrix products, arithmetic and copies ran while one was open for 6% -> 5% of each run, Pallas kernels for 22% -> 41%
where the time goes in v1:
time: 113 us
  Pallas kernels  56.7 us (50%)
  starting transfers between devices  25.9 us (23%)
  waiting for transfers between devices  17.8 us (16%)
  other arithmetic  5.31 us (5%)
  local copies, waits for them, and re-layouts  3.62 us (3%)
  between operations  2.43 us (2%)
    pallas_call x3, Pallas kernels, run_build(): pl.pallas_call(functools.partial(build_kernel, span), out_shape=jax.Shape...  27.9 us
    ppermute x26, starting transfers between devices, swap(): return lax.ppermute(x, axis, [(i, i ^ bit) for i in range(n)])  18.7 us
    ppermute x26, waiting for transfers between devices, swap(): return lax.ppermute(x, axis, [(i, i ^ bit) for i in range(n)])  17.8 us
    pallas_call x2, Pallas kernels, run_backward(): pl.pallas_call(functools.partial(backward_kernel, n, span), out_shape=jax...  11.8 us
    pallas_call x1, Pallas kernels, run_forward(): pl.pallas_call(functools.partial(forward_kernel, n, scale, span), out_sha...  10.4 us
    all_to_all x1, starting transfers between devices, shards(): lax.all_to_all(packed.reshape(n_col, stride, 128), 'col', split_axis=0, c...  7.23 us
    pallas_call x2, Pallas kernels, make_lists(): pl.pallas_call(functools.partial(list_kernel, keys, split, fills), out_sh...  3.3 us
    pallas_call x1, Pallas kernels, run_pack(): pl.pallas_call(functools.partial(pack_kernel, per, owners), out_shape=(ja...  3.26 us
  transfers between devices with their start and end apart: 27, of which 6 were waited for; matrix products, arithmetic and copies ran while one was open for 5% of the time, Pallas kernels for 41%

profile of v1, /device:TPU:9, one launch (start us, length us, event | category | flops | bytes accessed | tf_op | source)
XLA Modules:
  0.0 112.7 jit_solution(2540450363652511299)
XLA Ops:
  0.6 2.4 %collective-permute-start.5 = (bf16[4,128,128]{2,1,0:T(8,128)(2,1)}, bf16[4,128,128]{2,1,0:T(8,128)(2,1)S(1)}, u32[]{:S(2)}, u32[]{:S(2)}) collective-permute-start(bf16[4,128,128]{2,1,0:T(8,128)(2,1)} %bitcast.158), channel_id=1, source_target_pairs={{0,8},{1,9},{2,10},{3,11},{4,12},{5,13},{6,14},{7,15},{8,0},{9,1},... | collective-permute-start | bytes 393224 | tf_op jit(solution)/shard_map/ppermute | solution.py:14
  5.9 3.3 %shard_map.120 = (s32[1152,128]{1,0:T(8,128)}, s32[520,128]{1,0:T(8,128)S(1)}) custom-call(s32[1,1]{1,0:T(1,128)} %copy.62.count, s32[1,512]{1,0:T(1,128)} %bitcast.174, s32[1,512]{1,0:T(1,128)} %bitcast.171, s32[512,128]{1,0:T(8,128)S(1)} %bitcast.140, bf16[512,128]{1,0:T(8,128)(2,1)S(1)} %bitcast.141), custom_call_target="tpu_custom_call" | custom-call | tf_op jit(solution)/shard_map/pallas_call | solution.py:390
  9.1 7.2 %all-to-all-start = ((s32[16,72,128]{2,1,0:T(8,128)}), s32[16,72,128]{2,1,0:T(8,128)S(1)}, u32[]{:S(2)}, u32[]{:S(2)}) async-start(s32[16,72,128]{2,1,0:T(8,128)} %bitcast.23), calls=%async_computation | async-start | bytes 1179648 | tf_op jit(solution)/shard_map/all_to_all | solution.py:621
  17.2 1.0 pad_maximum_fusion.1.refs_0_
  19.0 1.2 %collective-permute-start.9 = (bf16[4,2,128,128]{3,2,1,0:T(8,128)(2,1)S(1)}, bf16[4,2,128,128]{3,2,1,0:T(8,128)(2,1)S(1)}, u32[]{:S(2)}, u32[]{:S(2)}) collective-permute-start(bf16[4,2,128,128]{3,2,1,0:T(8,128)(2,1)S(1)} %get-tuple-element.181), channel_id=1, source_target_pairs={{0,1},{1,0},{2,3},{3,2},{4,5},{5,4},{6,7},{7,6},{8,9},{9,8},{10,11... | collective-permute-start | bytes 786440 | tf_op jit(solution)/shard_map/ppermute | solution.py:14
  20.2 1.2 %collective-permute-start.8 = (bf16[4,2,128,128]{3,2,1,0:T(8,128)(2,1)S(1)}, bf16[4,2,128,128]{3,2,1,0:T(8,128)(2,1)S(1)}, u32[]{:S(2)}, u32[]{:S(2)}) collective-permute-start(bf16[4,2,128,128]{3,2,1,0:T(8,128)(2,1)S(1)} %get-tuple-element.182), channel_id=1, source_target_pairs={{0,2},{1,3},{2,0},{3,1},{4,6},{5,7},{6,4},{7,5},{8,10},{9,11},{10,... | collective-permute-start | bytes 786440 | tf_op jit(solution)/shard_map/ppermute | solution.py:14
  22.1 1.0 shard_map.122
  23.1 9.3 %shard_map.123.refs_1_ = bf16[672,128,128]{2,1,0:T(8,128)(2,1)} custom-call(s32[1,128]{1,0:T(1,128)S(1)} %get-tuple-element.88.marks, s32[2,672]{1,0:T(2,128)S(1)} %get-tuple-element.89.lists, s32[520,128]{1,0:T(8,128)S(1)} %get-tuple-element.90.codes, bf16[4,4,128,128]{3,2,1,0:T(8,128)(2,1)S(1)} %pad_maximum_fusion.1.refs_0_), custom_call_target="tpu_custom_call" | custom-call | flops 5637144576 | bytes 22020096 | tf_op jit(solution)/shard_map/pallas_call | solution.py:412
  32.7 1.8 %collective-permute-start.12 = (bf16[16,128,128]{2,1,0:T(8,128)(2,1)S(1)}, bf16[16,128,128]{2,1,0:T(8,128)(2,1)S(1)}, u32[]{:S(2)}, u32[]{:S(2)}) collective-permute-start(bf16[16,128,128]{2,1,0:T(8,128)(2,1)S(1)} %bitcast.135), channel_id=1, source_target_pairs={{0,16},{16,0},{1,17},{17,1},{2,18},{18,2},{3,19},{19,3},{4,20},{20... | collective-permute-start | bytes 1572872 | tf_op jit(solution)/shard_map/ppermute | solution.py:14
  34.9 2.3 %shard_map.121 = (s32[2,1088]{1,0:T(2,128)S(1)}, s32[1,256]{1,0:T(1,128)S(1)}, s32[1,128]{1,0:T(1,128)S(1)}) custom-call(s32[1,1024]{1,0:T(1,128)S(1)} %get-tuple-element.188.key_ref, s32[1,1024]{1,0:T(1,128)S(1)} %add.441.refs_0_, s32[1,1024]{1,0:T(1,128)S(1)} %get-tuple-element.187.refs_1_), custom_call_target="tpu_custom_call" | custom-call | flops 268435456 | bytes 1048576 | tf_op jit(solution)/shard_map/pallas_call | solution.py:526
  37.2 9.3 %shard_map.124.dense = bf16[1088,128,128]{2,1,0:T(8,128)(2,1)} custom-call(s32[1,128]{1,0:T(1,128)S(1)} %get-tuple-element.81.marks, s32[2,1088]{1,0:T(2,128)S(1)} %get-tuple-element.82.lists, s32[1152,128]{1,0:T(8,128)S(1)} %bitcast.131), custom_call_target="tpu_custom_call" | custom-call | flops 9126805504 | bytes 35651584 | tf_op jit(solution)/shard_map/pallas_call | solution.py:412
  47.5 1.0 collective-permute-done.4
  49.9 10.4 %shard_map.125 = (bf16[512,128]{1,0:T(8,128)(2,1)}, bf16[4,128,128]{2,1,0:T(8,128)(2,1)}, f32[136,128]{1,0:T(8,128)S(1)}) custom-call(s32[1,128]{1,0:T(1,128)S(1)} %get-tuple-element.81.marks, s32[2,1088]{1,0:T(2,128)S(1)} %get-tuple-element.82.lists, s32[1,256]{1,0:T(1,128)S(1)} %get-tuple-element.83.owner, bf16[128,128]{1,0:T(8,128)(2,1)S(1)} %copy-done.4, ...), custom_call_target="tpu_custom_call" | custom-call | flops 18253611008 | bytes 35651584 | tf_op jit(solution)/shard_map/pallas_call | solution.py:432
  60.7 2.5 %collective-permute-start.16 = (bf16[4,128,128]{2,1,0:T(8,128)(2,1)}, bf16[4,128,128]{2,1,0:T(8,128)(2,1)S(1)}, u32[]{:S(2)}, u32[]{:S(2)}) collective-permute-start(bf16[4,128,128]{2,1,0:T(8,128)(2,1)} %get-tuple-element.167.refs_0_), channel_id=1, source_target_pairs={{0,8},{1,9},{2,10},{3,11},{4,12},{5,13},{6,14},{7,15},{8,0},{9,1},... | collective-permute-start | bytes 393224 | tf_op jit(solution)/shard_map/ppermute | solution.py:14
  64.1 1.5 %collective-permute-start.20 = (f32[72,128]{1,0:T(8,128)S(1)}, f32[72,128]{1,0:T(8,128)S(1)}, u32[]{:S(2)}, u32[]{:S(2)}) collective-permute-start(f32[72,128]{1,0:T(8,128)S(1)} %fusion.26), channel_id=1, source_target_pairs={{0,1},{1,0},{2,3},{3,2},{4,5},{5,4},{6,7},{7,6},{8,9},{9,8},{10,11... | collective-permute-start | bytes 110600 | tf_op jit(solution)/shard_map/ppermute | solution.py:14
  65.7 9.3 %shard_map.126.dense = bf16[672,128,128]{2,1,0:T(8,128)(2,1)} custom-call(s32[1,128]{1,0:T(1,128)S(1)} %get-tuple-element.88.marks, s32[2,672]{1,0:T(2,128)S(1)} %get-tuple-element.89.lists, s32[520,128]{1,0:T(8,128)S(1)} %get-tuple-element.90.codes, bf16[4,128,128]{2,1,0:T(8,128)(2,1)} %get-tuple-element.167.refs_0_, ...), custom_call_target="tpu_custom_call", output_to_operand_aliasing={{}: (4, {})} | custom-call | flops 5637144576 | bytes 22020096 | tf_op jit(solution)/shard_map/pallas_call | solution.py:412
  75.1 2.8 %collective-permute-done.21 = f32[72,128]{1,0:T(8,128)S(1)} collective-permute-done((f32[72,128]{1,0:T(8,128)S(1)}, f32[72,128]{1,0:T(8,128)S(1)}, u32[]{:S(2)}, u32[]{:S(2)}) %collective-permute-start.21) | collective-permute-done | bytes 36896 | tf_op jit(solution)/shard_map/ppermute | solution.py:14
  79.7 3.1 %collective-permute-done.24 = f32[72,128]{1,0:T(8,128)S(1)} collective-permute-done((f32[72,128]{1,0:T(8,128)S(1)}, f32[72,128]{1,0:T(8,128)S(1)}, u32[]{:S(2)}, u32[]{:S(2)}) %collective-permute-start.24) | collective-permute-done | bytes 36896 | tf_op jit(solution)/shard_map/ppermute | solution.py:14
  82.8 4.3 %collective-permute-done.23 = bf16[4,2,128,128]{3,2,1,0:T(8,128)(2,1)S(1)} collective-permute-done((bf16[4,2,128,128]{3,2,1,0:T(8,128)(2,1)S(1)}, bf16[4,2,128,128]{3,2,1,0:T(8,128)(2,1)S(1)}, u32[]{:S(2)}, u32[]{:S(2)}) %collective-permute-start.23) | collective-permute-done | bytes 262176 | tf_op jit(solution)/shard_map/ppermute | solution.py:14
  87.2 1.7 %collective-permute-start.27 = (f32[72,128]{1,0:T(8,128)S(1)}, f32[72,128]{1,0:T(8,128)S(1)}, u32[]{:S(2)}, u32[]{:S(2)}) collective-permute-start(f32[72,128]{1,0:T(8,128)S(1)} %add.490), channel_id=1, source_target_pairs={{0,8},{1,9},{2,10},{3,11},{4,12},{5,13},{6,14},{7,15},{8,0},{9,1},... | collective-permute-start | bytes 110600 | tf_op jit(solution)/shard_map/ppermute | solution.py:14
  89.7 5.9 %shard_map.127.before = f32[8,128,128]{2,1,0:T(8,128)S(1)} custom-call(s32[1,128]{1,0:T(1,128)S(1)} %get-tuple-element.88.marks, s32[2,672]{1,0:T(2,128)S(1)} %get-tuple-element.89.lists, s32[1,128]{1,0:T(1,128)S(1)} %get-tuple-element.100.owner, f32[8,128,128]{2,1,0:T(8,128)S(1)} %broadcast_in_dim.32.before, bf16[672,128,128]{2,1,0:T(8,128)(2,1)} %shard_map.126.dense, ...), custom_call_target="tpu_custom_call" | custom-call | flops 11274289152 | bytes 22020096 | tf_op jit(solution)/shard_map/pallas_call | solution.py:458
  95.7 6.2 %collective-permute-done.25 = bf16[8,2,128,128]{3,2,1,0:T(8,128)(2,1)S(1)} collective-permute-done((bf16[8,2,128,128]{3,2,1,0:T(8,128)(2,1)S(1)}, bf16[8,2,128,128]{3,2,1,0:T(8,128)(2,1)S(1)}, u32[]{:S(2)}, u32[]{:S(2)}) %collective-permute-start.25) | collective-permute-done | bytes 524320 | tf_op jit(solution)/shard_map/ppermute | solution.py:14
  101.9 2.2 %collective-permute-start.29 = (f32[72,128]{1,0:T(8,128)S(1)}, f32[72,128]{1,0:T(8,128)S(1)}, u32[]{:S(2)}, u32[]{:S(2)}) collective-permute-start(f32[72,128]{1,0:T(8,128)S(1)} %add.491), channel_id=1, source_target_pairs={{0,16},{16,0},{1,17},{17,1},{2,18},{18,2},{3,19},{19,3},{4,20},{20... | collective-permute-start | bytes 110600 | tf_op jit(solution)/shard_map/ppermute | solution.py:14
  104.0 5.9 %shard_map.128 = f32[8,128,128]{2,1,0:T(8,128)S(1)} custom-call(s32[1,128]{1,0:T(1,128)S(1)} %get-tuple-element.88.marks, s32[2,672]{1,0:T(2,128)S(1)} %get-tuple-element.89.lists, s32[1,128]{1,0:T(1,128)S(1)} %get-tuple-element.100.owner, f32[8,128,128]{2,1,0:T(8,128)S(1)} %shard_map.127.before, bf16[672,128,128]{2,1,0:T(8,128)(2,1)} %shard_map.126.dense, ...), custom_call_target="tpu_custom_call" | custom-call | flops 11274289152 | bytes 22020096 | tf_op jit(solution)/shard_map/pallas_call | solution.py:458
  (97 shorter events, 13.5 us)
Async XLA Ops:
  0.6 16.6 %collective-permute-start.5 = (bf16[4,128,128]{2,1,0:T(8,128)(2,1)}, bf16[4,128,128]{2,1,0:T(8,128)(2,1)S(1)}, u32[]{:S(2)}, u32[]{:S(2)}) collective-permute-start(bf16[4,128,128]{2,1,0:T(8,128)(2,1)} %bitcast.158), channel_id=1, source_target_pairs={{0,8},{1,9},{2,10},{3,11},{4,12},{5,13},{6,14},{7,15},{8,0},{9,1},... | collective-permute-start | bytes 393224 | tf_op jit(solution)/shard_map/ppermute | solution.py:14
  3.0 14.2 %collective-permute-start.6 = (bf16[4,128,128]{2,1,0:T(8,128)(2,1)}, bf16[4,128,128]{2,1,0:T(8,128)(2,1)S(1)}, u32[]{:S(2)}, u32[]{:S(2)}) collective-permute-start(bf16[4,128,128]{2,1,0:T(8,128)(2,1)} %bitcast.159), channel_id=1, source_target_pairs={{0,4},{1,5},{2,6},{3,7},{4,0},{5,1},{6,2},{7,3},{8,12},{9,13},{10,... | collective-permute-start | bytes 393224 | tf_op jit(solution)/shard_map/ppermute | solution.py:14
  3.2 14.0 %collective-permute-start.7 = (bf16[4,128,128]{2,1,0:T(8,128)(2,1)}, bf16[4,128,128]{2,1,0:T(8,128)(2,1)S(1)}, u32[]{:S(2)}, u32[]{:S(2)}) collective-permute-start(bf16[4,128,128]{2,1,0:T(8,128)(2,1)} %bitcast.160), channel_id=1, source_target_pairs={{0,12},{1,13},{2,14},{3,15},{4,8},{5,9},{6,10},{7,11},{8,4},{9,5},... | collective-permute-start | bytes 393224 | tf_op jit(solution)/shard_map/ppermute | solution.py:14
  9.1 25.3 %all-to-all-start = ((s32[16,72,128]{2,1,0:T(8,128)}), s32[16,72,128]{2,1,0:T(8,128)S(1)}, u32[]{:S(2)}, u32[]{:S(2)}) async-start(s32[16,72,128]{2,1,0:T(8,128)} %bitcast.23), calls=%async_computation | async-start | bytes 1179648 | tf_op jit(solution)/shard_map/all_to_all | solution.py:621
  19.0 13.4 %collective-permute-start.9 = (bf16[4,2,128,128]{3,2,1,0:T(8,128)(2,1)S(1)}, bf16[4,2,128,128]{3,2,1,0:T(8,128)(2,1)S(1)}, u32[]{:S(2)}, u32[]{:S(2)}) collective-permute-start(bf16[4,2,128,128]{3,2,1,0:T(8,128)(2,1)S(1)} %get-tuple-element.181), channel_id=1, source_target_pairs={{0,1},{1,0},{2,3},{3,2},{4,5},{5,4},{6,7},{7,6},{8,9},{9,8},{10,11... | collective-permute-start | bytes 786440 | tf_op jit(solution)/shard_map/ppermute | solution.py:14
  20.2 12.2 %collective-permute-start.8 = (bf16[4,2,128,128]{3,2,1,0:T(8,128)(2,1)S(1)}, bf16[4,2,128,128]{3,2,1,0:T(8,128)(2,1)S(1)}, u32[]{:S(2)}, u32[]{:S(2)}) collective-permute-start(bf16[4,2,128,128]{3,2,1,0:T(8,128)(2,1)S(1)} %get-tuple-element.182), channel_id=1, source_target_pairs={{0,2},{1,3},{2,0},{3,1},{4,6},{5,7},{6,4},{7,5},{8,10},{9,11},{10,... | collective-permute-start | bytes 786440 | tf_op jit(solution)/shard_map/ppermute | solution.py:14
  32.5 14.0 %collective-permute-start.10 = (bf16[8,2,128,128]{3,2,1,0:T(8,128)(2,1)S(1)}, bf16[8,2,128,128]{3,2,1,0:T(8,128)(2,1)S(1)}, u32[]{:S(2)}, u32[]{:S(2)}) collective-permute-start(bf16[8,2,128,128]{3,2,1,0:T(8,128)(2,1)S(1)} %pad_maximum_fusion.2), channel_id=1, source_target_pairs={{0,1},{1,0},{2,3},{3,2},{4,5},{5,4},{6,7},{7,6},{8,9},{9,8},{10,11... | collective-permute-start | bytes 1572872 | tf_op jit(solution)/shard_map/ppermute | solution.py:14
  32.6 13.9 %collective-permute-start.11 = (bf16[8,2,128,128]{3,2,1,0:T(8,128)(2,1)S(1)}, bf16[8,2,128,128]{3,2,1,0:T(8,128)(2,1)S(1)}, u32[]{:S(2)}, u32[]{:S(2)}) collective-permute-start(bf16[8,2,128,128]{3,2,1,0:T(8,128)(2,1)S(1)} %pad_maximum_fusion.3), channel_id=1, source_target_pairs={{0,2},{1,3},{2,0},{3,1},{4,6},{5,7},{6,4},{7,5},{8,10},{9,11},{10,... | collective-permute-start | bytes 1572872 | tf_op jit(solution)/shard_map/ppermute | solution.py:14
  32.7 17.2 %collective-permute-start.12 = (bf16[16,128,128]{2,1,0:T(8,128)(2,1)S(1)}, bf16[16,128,128]{2,1,0:T(8,128)(2,1)S(1)}, u32[]{:S(2)}, u32[]{:S(2)}) collective-permute-start(bf16[16,128,128]{2,1,0:T(8,128)(2,1)S(1)} %bitcast.135), channel_id=1, source_target_pairs={{0,16},{16,0},{1,17},{17,1},{2,18},{18,2},{3,19},{19,3},{4,20},{20... | collective-permute-start | bytes 1572872 | tf_op jit(solution)/shard_map/ppermute | solution.py:14
  34.4 15.4 %collective-permute-start.14 = (bf16[16,128,128]{2,1,0:T(8,128)(2,1)S(1)}, bf16[16,128,128]{2,1,0:T(8,128)(2,1)}, u32[]{:S(2)}, u32[]{:S(2)}) collective-permute-start(bf16[16,128,128]{2,1,0:T(8,128)(2,1)S(1)} %bitcast.133), channel_id=1, source_target_pairs={{0,16},{16,0},{1,17},{17,1},{2,18},{18,2},{3,19},{19,3},{4,20},{20... | collective-permute-start | bytes 1572872 | tf_op jit(solution)/shard_map/ppermute | solution.py:14
  46.6 3.3 %collective-permute-start.13 = (bf16[16,128,128]{2,1,0:T(8,128)(2,1)S(1)}, bf16[16,128,128]{2,1,0:T(8,128)(2,1)S(1)}, u32[]{:S(2)}, u32[]{:S(2)}) collective-permute-start(bf16[16,128,128]{2,1,0:T(8,128)(2,1)S(1)} %bitcast.144), channel_id=1, source_target_pairs={{0,16},{16,0},{1,17},{17,1},{2,18},{18,2},{3,19},{19,3},{4,20},{20... | collective-permute-start | bytes 1572872 | tf_op jit(solution)/shard_map/ppermute | solution.py:14
  60.6 3.5 %collective-permute-start.19 = (f32[1,72,128]{2,1,0:T(8,128)S(1)}, f32[1,72,128]{2,1,0:T(8,128)S(1)}, u32[]{:S(2)}, u32[]{:S(2)}) collective-permute-start(f32[1,72,128]{2,1,0:T(8,128)S(1)} %slice_bitcast_fusion.10), channel_id=1, source_target_pairs={{0,16},{16,0},{1,17},{17,1},{2,18},{18,2},{3,19},{19,3},{4,20},{20... | collective-permute-start | bytes 110600 | tf_op jit(solution)/shard_map/ppermute | solution.py:14
  60.7 17.2 %collective-permute-start.16 = (bf16[4,128,128]{2,1,0:T(8,128)(2,1)}, bf16[4,128,128]{2,1,0:T(8,128)(2,1)S(1)}, u32[]{:S(2)}, u32[]{:S(2)}) collective-permute-start(bf16[4,128,128]{2,1,0:T(8,128)(2,1)} %get-tuple-element.167.refs_0_), channel_id=1, source_target_pairs={{0,8},{1,9},{2,10},{3,11},{4,12},{5,13},{6,14},{7,15},{8,0},{9,1},... | collective-permute-start | bytes 393224 | tf_op jit(solution)/shard_map/ppermute | solution.py:14
  63.2 14.7 %collective-permute-start.17 = (bf16[4,128,128]{2,1,0:T(8,128)(2,1)}, bf16[4,128,128]{2,1,0:T(8,128)(2,1)S(1)}, u32[]{:S(2)}, u32[]{:S(2)}) collective-permute-start(bf16[4,128,128]{2,1,0:T(8,128)(2,1)} %get-tuple-element.167.refs_0_), channel_id=1, source_target_pairs={{0,4},{1,5},{2,6},{3,7},{4,0},{5,1},{6,2},{7,3},{8,12},{9,13},{10,... | collective-permute-start | bytes 393224 | tf_op jit(solution)/shard_map/ppermute | solution.py:14
  64.1 13.8 %collective-permute-start.18 = (bf16[4,128,128]{2,1,0:T(8,128)(2,1)}, bf16[4,128,128]{2,1,0:T(8,128)(2,1)S(1)}, u32[]{:S(2)}, u32[]{:S(2)}) collective-permute-start(bf16[4,128,128]{2,1,0:T(8,128)(2,1)} %get-tuple-element.167.refs_0_), channel_id=1, source_target_pairs={{0,12},{1,13},{2,14},{3,15},{4,8},{5,9},{6,10},{7,11},{8,4},{9,5},... | collective-permute-start | bytes 393224 | tf_op jit(solution)/shard_map/ppermute | solution.py:14
  64.1 10.8 %collective-permute-start.20 = (f32[72,128]{1,0:T(8,128)S(1)}, f32[72,128]{1,0:T(8,128)S(1)}, u32[]{:S(2)}, u32[]{:S(2)}) collective-permute-start(f32[72,128]{1,0:T(8,128)S(1)} %fusion.26), channel_id=1, source_target_pairs={{0,1},{1,0},{2,3},{3,2},{4,5},{5,4},{6,7},{7,6},{8,9},{9,8},{10,11... | collective-permute-start | bytes 110600 | tf_op jit(solution)/shard_map/ppermute | solution.py:14
  75.0 2.9 %collective-permute-start.21 = (f32[72,128]{1,0:T(8,128)S(1)}, f32[72,128]{1,0:T(8,128)S(1)}, u32[]{:S(2)}, u32[]{:S(2)}) collective-permute-start(f32[72,128]{1,0:T(8,128)S(1)} %add.488), channel_id=1, source_target_pairs={{0,2},{1,3},{2,0},{3,1},{4,6},{5,7},{6,4},{7,5},{8,10},{9,11},{10,... | collective-permute-start | bytes 110600 | tf_op jit(solution)/shard_map/ppermute | solution.py:14
  78.9 8.1 %collective-permute-start.23 = (bf16[4,2,128,128]{3,2,1,0:T(8,128)(2,1)S(1)}, bf16[4,2,128,128]{3,2,1,0:T(8,128)(2,1)S(1)}, u32[]{:S(2)}, u32[]{:S(2)}) collective-permute-start(bf16[4,2,128,128]{3,2,1,0:T(8,128)(2,1)S(1)} %get-tuple-element.179), channel_id=1, source_target_pairs={{0,1},{1,0},{2,3},{3,2},{4,5},{5,4},{6,7},{7,6},{8,9},{9,8},{10,11... | collective-permute-start | bytes 786440 | tf_op jit(solution)/shard_map/ppermute | solution.py:14
  79.0 8.1 %collective-permute-start.22 = (bf16[4,2,128,128]{3,2,1,0:T(8,128)(2,1)S(1)}, bf16[4,2,128,128]{3,2,1,0:T(8,128)(2,1)S(1)}, u32[]{:S(2)}, u32[]{:S(2)}) collective-permute-start(bf16[4,2,128,128]{3,2,1,0:T(8,128)(2,1)S(1)} %get-tuple-element.180), channel_id=1, source_target_pairs={{0,2},{1,3},{2,0},{3,1},{4,6},{5,7},{6,4},{7,5},{8,10},{9,11},{10,... | collective-permute-start | bytes 786440 | tf_op jit(solution)/shard_map/ppermute | solution.py:14
  79.6 3.1 %collective-permute-start.24 = (f32[72,128]{1,0:T(8,128)S(1)}, f32[72,128]{1,0:T(8,128)S(1)}, u32[]{:S(2)}, u32[]{:S(2)}) collective-permute-start(f32[72,128]{1,0:T(8,128)S(1)} %add.489), channel_id=1, source_target_pairs={{0,4},{1,5},{2,6},{3,7},{4,0},{5,1},{6,2},{7,3},{8,12},{9,13},{10,... | collective-permute-start | bytes 110600 | tf_op jit(solution)/shard_map/ppermute | solution.py:14
  87.2 8.5 %collective-permute-start.27 = (f32[72,128]{1,0:T(8,128)S(1)}, f32[72,128]{1,0:T(8,128)S(1)}, u32[]{:S(2)}, u32[]{:S(2)}) collective-permute-start(f32[72,128]{1,0:T(8,128)S(1)} %add.490), channel_id=1, source_target_pairs={{0,8},{1,9},{2,10},{3,11},{4,12},{5,13},{6,14},{7,15},{8,0},{9,1},... | collective-permute-start | bytes 110600 | tf_op jit(solution)/shard_map/ppermute | solution.py:14
  88.9 13.0 %collective-permute-start.25 = (bf16[8,2,128,128]{3,2,1,0:T(8,128)(2,1)S(1)}, bf16[8,2,128,128]{3,2,1,0:T(8,128)(2,1)S(1)}, u32[]{:S(2)}, u32[]{:S(2)}) collective-permute-start(bf16[8,2,128,128]{3,2,1,0:T(8,128)(2,1)S(1)} %pad_maximum_fusion.5), channel_id=1, source_target_pairs={{0,1},{1,0},{2,3},{3,2},{4,5},{5,4},{6,7},{7,6},{8,9},{9,8},{10,11... | collective-permute-start | bytes 1572872 | tf_op jit(solution)/shard_map/ppermute | solution.py:14
  89.7 12.2 %collective-permute-start.26 = (bf16[8,2,128,128]{3,2,1,0:T(8,128)(2,1)S(1)}, bf16[8,2,128,128]{3,2,1,0:T(8,128)(2,1)S(1)}, u32[]{:S(2)}, u32[]{:S(2)}) collective-permute-start(bf16[8,2,128,128]{3,2,1,0:T(8,128)(2,1)S(1)} %pad_maximum_fusion.6), channel_id=1, source_target_pairs={{0,2},{1,3},{2,0},{3,1},{4,6},{5,7},{6,4},{7,5},{8,10},{9,11},{10,... | collective-permute-start | bytes 1572872 | tf_op jit(solution)/shard_map/ppermute | solution.py:14
  101.9 8.5 %collective-permute-start.29 = (f32[72,128]{1,0:T(8,128)S(1)}, f32[72,128]{1,0:T(8,128)S(1)}, u32[]{:S(2)}, u32[]{:S(2)}) collective-permute-start(f32[72,128]{1,0:T(8,128)S(1)} %add.491), channel_id=1, source_target_pairs={{0,16},{16,0},{1,17},{17,1},{2,18},{18,2},{3,19},{19,3},{4,20},{20... | collective-permute-start | bytes 110600 | tf_op jit(solution)/shard_map/ppermute | solution.py:14
  (8 other events, 41.4 us)

commit v2 on v1

--- a/solution.py
+++ b/solution.py
@@ -682,10 +682,13 @@
         held, state["total"], state["dense"] = lax.optimization_barrier(
             (held, state["total"], state["dense"])
         )
+        if step == 1:
+            add_products(0, held)
+            state["acc"], state["total"] = lax.optimization_barrier(
+                (state["acc"], state["total"])
+            )
         if steps:
             add_total()
-        if step == 1:
-            add_products(0, held)
         return held
 
     def add_products(half, pieces):

time: 113 us -> 115 us (1.018)
  the two profiles are of different devices: /device:TPU:9 before, /device:TPU:0 now
where the time goes in v2:
time: 115 us
  Pallas kernels  44.8 us (39%)
  starting transfers between devices  40.9 us (36%)
  waiting for transfers between devices  16.5 us (14%)
  other arithmetic  5.3 us (5%)
  local copies, waits for them, and re-layouts  3.63 us (3%)
  between operations  2.35 us (2%)
    ppermute x26, starting transfers between devices, swap(): return lax.ppermute(x, axis, [(i, i ^ bit) for i in range(n)])  34 us
    pallas_call x3, Pallas kernels, run_build(): pl.pallas_call(functools.partial(build_kernel, span), out_shape=jax.Shape...  20.4 us
    ppermute x26, waiting for transfers between devices, swap(): return lax.ppermute(x, axis, [(i, i ^ bit) for i in range(n)])  16.5 us
    pallas_call x1, Pallas kernels, run_forward(): pl.pallas_call(functools.partial(forward_kernel, n, scale, span), out_sha...  9.88 us
    pallas_call x2, Pallas kernels, run_backward(): pl.pallas_call(functools.partial(backward_kernel, n, span), out_shape=jax...  8.35 us
    all_to_all x1, starting transfers between devices, shards(): lax.all_to_all(packed.reshape(n_col, stride, 128), 'col', split_axis=0, c...  6.86 us
    pallas_call x2, Pallas kernels, make_lists(): pl.pallas_call(functools.partial(list_kernel, keys, split, fills), out_sh...  3.3 us
    pallas_call x1, Pallas kernels, run_pack(): pl.pallas_call(functools.partial(pack_kernel, per, owners), out_shape=(ja...  2.94 us
  transfers between devices with their start and end apart: 27, of which 9 were waited for; matrix products, arithmetic and copies ran while one was open for 5% of the time, Pallas kernels for 31%

profile of v2, /device:TPU:0, one launch (start us, length us, event | category | flops | bytes accessed | tf_op | source)
XLA Modules:
  0.0 114.6 jit_solution(12436358187209495962)
XLA Ops:
  0.6 4.1 %collective-permute-start.5 = (bf16[4,128,128]{2,1,0:T(8,128)(2,1)}, bf16[4,128,128]{2,1,0:T(8,128)(2,1)S(1)}, u32[]{:S(2)}, u32[]{:S(2)}) collective-permute-start(bf16[4,128,128]{2,1,0:T(8,128)(2,1)} %bitcast.158), channel_id=1, source_target_pairs={{0,8},{1,9},{2,10},{3,11},{4,12},{5,13},{6,14},{7,15},{8,0},{9,1},... | collective-permute-start | bytes 393224 | tf_op jit(solution)/shard_map/ppermute | solution.py:14
  8.8 2.9 %shard_map.120 = (s32[1152,128]{1,0:T(8,128)}, s32[520,128]{1,0:T(8,128)S(1)}) custom-call(s32[1,1]{1,0:T(1,128)} %copy.62.count, s32[1,512]{1,0:T(1,128)} %bitcast.174, s32[1,512]{1,0:T(1,128)} %bitcast.171, s32[512,128]{1,0:T(8,128)S(1)} %bitcast.140, bf16[512,128]{1,0:T(8,128)(2,1)S(1)} %bitcast.141), custom_call_target="tpu_custom_call" | custom-call | tf_op jit(solution)/shard_map/pallas_call | solution.py:390
  11.8 6.9 %all-to-all-start = ((s32[16,72,128]{2,1,0:T(8,128)}), s32[16,72,128]{2,1,0:T(8,128)S(1)}, u32[]{:S(2)}, u32[]{:S(2)}) async-start(s32[16,72,128]{2,1,0:T(8,128)} %bitcast.23), calls=%async_computation | async-start | bytes 1179648 | tf_op jit(solution)/shard_map/all_to_all | solution.py:621
  21.2 2.0 %collective-permute-start.9 = (bf16[4,2,128,128]{3,2,1,0:T(8,128)(2,1)S(1)}, bf16[4,2,128,128]{3,2,1,0:T(8,128)(2,1)S(1)}, u32[]{:S(2)}, u32[]{:S(2)}) collective-permute-start(bf16[4,2,128,128]{3,2,1,0:T(8,128)(2,1)S(1)} %get-tuple-element.185), channel_id=1, source_target_pairs={{0,1},{1,0},{2,3},{3,2},{4,5},{5,4},{6,7},{7,6},{8,9},{9,8},{10,11... | collective-permute-start | bytes 786440 | tf_op jit(solution)/shard_map/ppermute | solution.py:14
  26.4 5.9 %shard_map.123.refs_1_ = bf16[672,128,128]{2,1,0:T(8,128)(2,1)} custom-call(s32[1,128]{1,0:T(1,128)S(1)} %get-tuple-element.90.marks, s32[2,672]{1,0:T(2,128)S(1)} %get-tuple-element.91.lists, s32[520,128]{1,0:T(8,128)S(1)} %get-tuple-element.92.codes, bf16[4,4,128,128]{3,2,1,0:T(8,128)(2,1)S(1)} %pad_maximum_fusion.1.refs_0_), custom_call_target="tpu_custom_call" | custom-call | flops 5637144576 | bytes 22020096 | tf_op jit(solution)/shard_map/pallas_call | solution.py:412
  32.6 1.8 %collective-permute-start.10 = (bf16[8,2,128,128]{3,2,1,0:T(8,128)(2,1)S(1)}, bf16[8,2,128,128]{3,2,1,0:T(8,128)(2,1)S(1)}, u32[]{:S(2)}, u32[]{:S(2)}) collective-permute-start(bf16[8,2,128,128]{3,2,1,0:T(8,128)(2,1)S(1)} %pad_maximum_fusion.2), channel_id=1, source_target_pairs={{0,1},{1,0},{2,3},{3,2},{4,5},{5,4},{6,7},{7,6},{8,9},{9,8},{10,11... | collective-permute-start | bytes 1572872 | tf_op jit(solution)/shard_map/ppermute | solution.py:14
  34.4 2.2 %collective-permute-start.11 = (bf16[8,2,128,128]{3,2,1,0:T(8,128)(2,1)S(1)}, bf16[8,2,128,128]{3,2,1,0:T(8,128)(2,1)S(1)}, u32[]{:S(2)}, u32[]{:S(2)}) collective-permute-start(bf16[8,2,128,128]{3,2,1,0:T(8,128)(2,1)S(1)} %pad_maximum_fusion.3), channel_id=1, source_target_pairs={{0,2},{1,3},{2,0},{3,1},{4,6},{5,7},{6,4},{7,5},{8,10},{9,11},{10,... | collective-permute-start | bytes 1572872 | tf_op jit(solution)/shard_map/ppermute | solution.py:14
  37.5 2.3 %shard_map.121 = (s32[2,1088]{1,0:T(2,128)S(1)}, s32[1,256]{1,0:T(1,128)S(1)}, s32[1,128]{1,0:T(1,128)S(1)}) custom-call(s32[1,1024]{1,0:T(1,128)S(1)} %get-tuple-element.192.key_ref, s32[1,1024]{1,0:T(1,128)S(1)} %add.441.refs_0_, s32[1,1024]{1,0:T(1,128)S(1)} %get-tuple-element.191.refs_1_), custom_call_target="tpu_custom_call" | custom-call | flops 268435456 | bytes 1048576 | tf_op jit(solution)/shard_map/pallas_call | solution.py:526
  39.8 8.6 %shard_map.124.dense = bf16[1088,128,128]{2,1,0:T(8,128)(2,1)} custom-call(s32[1,128]{1,0:T(1,128)S(1)} %get-tuple-element.83.marks, s32[2,1088]{1,0:T(2,128)S(1)} %get-tuple-element.84.lists, s32[1152,128]{1,0:T(8,128)S(1)} %bitcast.131), custom_call_target="tpu_custom_call" | custom-call | flops 9126805504 | bytes 35651584 | tf_op jit(solution)/shard_map/pallas_call | solution.py:412
  52.1 9.9 %shard_map.125 = (bf16[512,128]{1,0:T(8,128)(2,1)}, bf16[4,128,128]{2,1,0:T(8,128)(2,1)}, f32[136,128]{1,0:T(8,128)S(1)}) custom-call(s32[1,128]{1,0:T(1,128)S(1)} %get-tuple-element.83.marks, s32[2,1088]{1,0:T(2,128)S(1)} %get-tuple-element.84.lists, s32[1,256]{1,0:T(1,128)S(1)} %get-tuple-element.85.owner, bf16[128,128]{1,0:T(8,128)(2,1)S(1)} %copy-done.4, ...), custom_call_target="tpu_custom_call" | custom-call | flops 18253611008 | bytes 35651584 | tf_op jit(solution)/shard_map/pallas_call | solution.py:432
  64.5 1.8 %collective-permute-start.17 = (bf16[4,128,128]{2,1,0:T(8,128)(2,1)}, bf16[4,128,128]{2,1,0:T(8,128)(2,1)S(1)}, u32[]{:S(2)}, u32[]{:S(2)}) collective-permute-start(bf16[4,128,128]{2,1,0:T(8,128)(2,1)} %get-tuple-element.171.refs_0_), channel_id=1, source_target_pairs={{0,4},{1,5},{2,6},{3,7},{4,0},{5,1},{6,2},{7,3},{8,12},{9,13},{10,... | collective-permute-start | bytes 393224 | tf_op jit(solution)/shard_map/ppermute | solution.py:14
  67.7 2.0 %collective-permute-start.20 = (f32[72,128]{1,0:T(8,128)S(1)}, f32[72,128]{1,0:T(8,128)S(1)}, u32[]{:S(2)}, u32[]{:S(2)}) collective-permute-start(f32[72,128]{1,0:T(8,128)S(1)} %fusion.26), channel_id=1, source_target_pairs={{0,1},{1,0},{2,3},{3,2},{4,5},{5,4},{6,7},{7,6},{8,9},{9,8},{10,11... | collective-permute-start | bytes 110600 | tf_op jit(solution)/shard_map/ppermute | solution.py:14
  69.7 5.9 %shard_map.126.dense = bf16[672,128,128]{2,1,0:T(8,128)(2,1)} custom-call(s32[1,128]{1,0:T(1,128)S(1)} %get-tuple-element.90.marks, s32[2,672]{1,0:T(2,128)S(1)} %get-tuple-element.91.lists, s32[520,128]{1,0:T(8,128)S(1)} %get-tuple-element.92.codes, bf16[4,128,128]{2,1,0:T(8,128)(2,1)} %get-tuple-element.171.refs_0_, ...), custom_call_target="tpu_custom_call", output_to_operand_aliasing={{}: (4, {})} | custom-call | flops 5637144576 | bytes 22020096 | tf_op jit(solution)/shard_map/pallas_call | solution.py:412
  75.6 2.3 %collective-permute-start.21 = (f32[72,128]{1,0:T(8,128)S(1)}, f32[72,128]{1,0:T(8,128)S(1)}, u32[]{:S(2)}, u32[]{:S(2)}) collective-permute-start(f32[72,128]{1,0:T(8,128)S(1)} %add.488), channel_id=1, source_target_pairs={{0,2},{1,3},{2,0},{3,1},{4,6},{5,7},{6,4},{7,5},{8,10},{9,11},{10,... | collective-permute-start | bytes 110600 | tf_op jit(solution)/shard_map/ppermute | solution.py:14
  77.9 1.9 %collective-permute-done.21 = f32[72,128]{1,0:T(8,128)S(1)} collective-permute-done((f32[72,128]{1,0:T(8,128)S(1)}, f32[72,128]{1,0:T(8,128)S(1)}, u32[]{:S(2)}, u32[]{:S(2)}) %collective-permute-start.21) | collective-permute-done | bytes 36896 | tf_op jit(solution)/shard_map/ppermute | solution.py:14
  82.0 2.0 %collective-permute-start.22 = (bf16[4,2,128,128]{3,2,1,0:T(8,128)(2,1)S(1)}, bf16[4,2,128,128]{3,2,1,0:T(8,128)(2,1)S(1)}, u32[]{:S(2)}, u32[]{:S(2)}) collective-permute-start(bf16[4,2,128,128]{3,2,1,0:T(8,128)(2,1)S(1)} %get-tuple-element.184), channel_id=1, source_target_pairs={{0,2},{1,3},{2,0},{3,1},{4,6},{5,7},{6,4},{7,5},{8,10},{9,11},{10,... | collective-permute-start | bytes 786440 | tf_op jit(solution)/shard_map/ppermute | solution.py:14
  84.4 3.6 %collective-permute-done.24 = f32[72,128]{1,0:T(8,128)S(1)} collective-permute-done((f32[72,128]{1,0:T(8,128)S(1)}, f32[72,128]{1,0:T(8,128)S(1)}, u32[]{:S(2)}, u32[]{:S(2)}) %collective-permute-start.24) | collective-permute-done | bytes 36896 | tf_op jit(solution)/shard_map/ppermute | solution.py:14
  88.0 2.0 %collective-permute-done.23 = bf16[4,2,128,128]{3,2,1,0:T(8,128)(2,1)S(1)} collective-permute-done((bf16[4,2,128,128]{3,2,1,0:T(8,128)(2,1)S(1)}, bf16[4,2,128,128]{3,2,1,0:T(8,128)(2,1)S(1)}, u32[]{:S(2)}, u32[]{:S(2)}) %collective-permute-start.23) | collective-permute-done | bytes 262176 | tf_op jit(solution)/shard_map/ppermute | solution.py:14
  90.4 1.7 %collective-permute-start.25 = (bf16[8,2,128,128]{3,2,1,0:T(8,128)(2,1)S(1)}, bf16[8,2,128,128]{3,2,1,0:T(8,128)(2,1)S(1)}, u32[]{:S(2)}, u32[]{:S(2)}) collective-permute-start(bf16[8,2,128,128]{3,2,1,0:T(8,128)(2,1)S(1)} %pad_maximum_fusion.5), channel_id=1, source_target_pairs={{0,1},{1,0},{2,3},{3,2},{4,5},{5,4},{6,7},{7,6},{8,9},{9,8},{10,11... | collective-permute-start | bytes 1572872 | tf_op jit(solution)/shard_map/ppermute | solution.py:14
  92.5 4.2 %shard_map.127.before = f32[8,128,128]{2,1,0:T(8,128)S(1)} custom-call(s32[1,128]{1,0:T(1,128)S(1)} %get-tuple-element.90.marks, s32[2,672]{1,0:T(2,128)S(1)} %get-tuple-element.91.lists, s32[1,128]{1,0:T(1,128)S(1)} %get-tuple-element.102.owner, f32[8,128,128]{2,1,0:T(8,128)S(1)} %broadcast_in_dim.32.before, bf16[672,128,128]{2,1,0:T(8,128)(2,1)} %shard_map.126.dense, ...), custom_call_target="tpu_custom_call" | custom-call | flops 11274289152 | bytes 22020096 | tf_op jit(solution)/shard_map/pallas_call | solution.py:458
  98.3 3.5 %collective-permute-done.27 = f32[72,128]{1,0:T(8,128)S(1)} collective-permute-done((f32[72,128]{1,0:T(8,128)S(1)}, f32[72,128]{1,0:T(8,128)S(1)}, u32[]{:S(2)}, u32[]{:S(2)}) %collective-permute-start.27) | collective-permute-done | bytes 36896 | tf_op jit(solution)/shard_map/ppermute | solution.py:14
  101.8 2.5 %collective-permute-done.25 = bf16[8,2,128,128]{3,2,1,0:T(8,128)(2,1)S(1)} collective-permute-done((bf16[8,2,128,128]{3,2,1,0:T(8,128)(2,1)S(1)}, bf16[8,2,128,128]{3,2,1,0:T(8,128)(2,1)S(1)}, u32[]{:S(2)}, u32[]{:S(2)}) %collective-permute-start.25) | collective-permute-done | bytes 524320 | tf_op jit(solution)/shard_map/ppermute | solution.py:14
  105.7 4.2 %shard_map.128 = f32[8,128,128]{2,1,0:T(8,128)S(1)} custom-call(s32[1,128]{1,0:T(1,128)S(1)} %get-tuple-element.90.marks, s32[2,672]{1,0:T(2,128)S(1)} %get-tuple-element.91.lists, s32[1,128]{1,0:T(1,128)S(1)} %get-tuple-element.102.owner, f32[8,128,128]{2,1,0:T(8,128)S(1)} %shard_map.127.before, bf16[672,128,128]{2,1,0:T(8,128)(2,1)} %shard_map.126.dense, ...), custom_call_target="tpu_custom_call" | custom-call | flops 11274289152 | bytes 22020096 | tf_op jit(solution)/shard_map/pallas_call | solution.py:458
  110.2 2.3 %collective-permute-start.28 = (f32[1,512,128]{2,1,0:T(8,128)S(1)}, f32[1,512,128]{2,1,0:T(8,128)S(1)}, u32[]{:S(2)}, u32[]{:S(2)}) collective-permute-start(f32[1,512,128]{2,1,0:T(8,128)S(1)} %slice_bitcast_fusion.8), channel_id=1, source_target_pairs={{0,16},{16,0},{1,17},{17,1},{2,18},{18,2},{3,19},{19,3},{4,20},{20... | collective-permute-start | bytes 786440 | tf_op jit(solution)/shard_map/ppermute | solution.py:14
  (97 shorter events, 25.9 us)
Async XLA Ops:
  0.6 18.8 %collective-permute-start.5 = (bf16[4,128,128]{2,1,0:T(8,128)(2,1)}, bf16[4,128,128]{2,1,0:T(8,128)(2,1)S(1)}, u32[]{:S(2)}, u32[]{:S(2)}) collective-permute-start(bf16[4,128,128]{2,1,0:T(8,128)(2,1)} %bitcast.158), channel_id=1, source_target_pairs={{0,8},{1,9},{2,10},{3,11},{4,12},{5,13},{6,14},{7,15},{8,0},{9,1},... | collective-permute-start | bytes 393224 | tf_op jit(solution)/shard_map/ppermute | solution.py:14
  4.7 14.7 %collective-permute-start.6 = (bf16[4,128,128]{2,1,0:T(8,128)(2,1)}, bf16[4,128,128]{2,1,0:T(8,128)(2,1)S(1)}, u32[]{:S(2)}, u32[]{:S(2)}) collective-permute-start(bf16[4,128,128]{2,1,0:T(8,128)(2,1)} %bitcast.159), channel_id=1, source_target_pairs={{0,4},{1,5},{2,6},{3,7},{4,0},{5,1},{6,2},{7,3},{8,12},{9,13},{10,... | collective-permute-start | bytes 393224 | tf_op jit(solution)/shard_map/ppermute | solution.py:14
  6.3 13.2 %collective-permute-start.7 = (bf16[4,128,128]{2,1,0:T(8,128)(2,1)}, bf16[4,128,128]{2,1,0:T(8,128)(2,1)S(1)}, u32[]{:S(2)}, u32[]{:S(2)}) collective-permute-start(bf16[4,128,128]{2,1,0:T(8,128)(2,1)} %bitcast.160), channel_id=1, source_target_pairs={{0,12},{1,13},{2,14},{3,15},{4,8},{5,9},{6,10},{7,11},{8,4},{9,5},... | collective-permute-start | bytes 393224 | tf_op jit(solution)/shard_map/ppermute | solution.py:14
  11.8 25.3 %all-to-all-start = ((s32[16,72,128]{2,1,0:T(8,128)}), s32[16,72,128]{2,1,0:T(8,128)S(1)}, u32[]{:S(2)}, u32[]{:S(2)}) async-start(s32[16,72,128]{2,1,0:T(8,128)} %bitcast.23), calls=%async_computation | async-start | bytes 1179648 | tf_op jit(solution)/shard_map/all_to_all | solution.py:621
  21.2 11.2 %collective-permute-start.9 = (bf16[4,2,128,128]{3,2,1,0:T(8,128)(2,1)S(1)}, bf16[4,2,128,128]{3,2,1,0:T(8,128)(2,1)S(1)}, u32[]{:S(2)}, u32[]{:S(2)}) collective-permute-start(bf16[4,2,128,128]{3,2,1,0:T(8,128)(2,1)S(1)} %get-tuple-element.185), channel_id=1, source_target_pairs={{0,1},{1,0},{2,3},{3,2},{4,5},{5,4},{6,7},{7,6},{8,9},{9,8},{10,11... | collective-permute-start | bytes 786440 | tf_op jit(solution)/shard_map/ppermute | solution.py:14
  23.2 9.3 %collective-permute-start.8 = (bf16[4,2,128,128]{3,2,1,0:T(8,128)(2,1)S(1)}, bf16[4,2,128,128]{3,2,1,0:T(8,128)(2,1)S(1)}, u32[]{:S(2)}, u32[]{:S(2)}) collective-permute-start(bf16[4,2,128,128]{3,2,1,0:T(8,128)(2,1)S(1)} %get-tuple-element.186), channel_id=1, source_target_pairs={{0,2},{1,3},{2,0},{3,1},{4,6},{5,7},{6,4},{7,5},{8,10},{9,11},{10,... | collective-permute-start | bytes 786440 | tf_op jit(solution)/shard_map/ppermute | solution.py:14
  32.6 15.8 %collective-permute-start.10 = (bf16[8,2,128,128]{3,2,1,0:T(8,128)(2,1)S(1)}, bf16[8,2,128,128]{3,2,1,0:T(8,128)(2,1)S(1)}, u32[]{:S(2)}, u32[]{:S(2)}) collective-permute-start(bf16[8,2,128,128]{3,2,1,0:T(8,128)(2,1)S(1)} %pad_maximum_fusion.2), channel_id=1, source_target_pairs={{0,1},{1,0},{2,3},{3,2},{4,5},{5,4},{6,7},{7,6},{8,9},{9,8},{10,11... | collective-permute-start | bytes 1572872 | tf_op jit(solution)/shard_map/ppermute | solution.py:14
  34.4 14.0 %collective-permute-start.11 = (bf16[8,2,128,128]{3,2,1,0:T(8,128)(2,1)S(1)}, bf16[8,2,128,128]{3,2,1,0:T(8,128)(2,1)S(1)}, u32[]{:S(2)}, u32[]{:S(2)}) collective-permute-start(bf16[8,2,128,128]{3,2,1,0:T(8,128)(2,1)S(1)} %pad_maximum_fusion.3), channel_id=1, source_target_pairs={{0,2},{1,3},{2,0},{3,1},{4,6},{5,7},{6,4},{7,5},{8,10},{9,11},{10,... | collective-permute-start | bytes 1572872 | tf_op jit(solution)/shard_map/ppermute | solution.py:14
  36.5 15.5 %collective-permute-start.12 = (bf16[16,128,128]{2,1,0:T(8,128)(2,1)S(1)}, bf16[16,128,128]{2,1,0:T(8,128)(2,1)S(1)}, u32[]{:S(2)}, u32[]{:S(2)}) collective-permute-start(bf16[16,128,128]{2,1,0:T(8,128)(2,1)S(1)} %bitcast.135), channel_id=1, source_target_pairs={{0,16},{16,0},{1,17},{17,1},{2,18},{18,2},{3,19},{19,3},{4,20},{20... | collective-permute-start | bytes 1572872 | tf_op jit(solution)/shard_map/ppermute | solution.py:14
  36.5 15.5 %collective-permute-start.14 = (bf16[16,128,128]{2,1,0:T(8,128)(2,1)S(1)}, bf16[16,128,128]{2,1,0:T(8,128)(2,1)}, u32[]{:S(2)}, u32[]{:S(2)}) collective-permute-start(bf16[16,128,128]{2,1,0:T(8,128)(2,1)S(1)} %bitcast.133), channel_id=1, source_target_pairs={{0,16},{16,0},{1,17},{17,1},{2,18},{18,2},{3,19},{19,3},{4,20},{20... | collective-permute-start | bytes 1572872 | tf_op jit(solution)/shard_map/ppermute | solution.py:14
  48.4 3.7 %collective-permute-start.13 = (bf16[16,128,128]{2,1,0:T(8,128)(2,1)S(1)}, bf16[16,128,128]{2,1,0:T(8,128)(2,1)S(1)}, u32[]{:S(2)}, u32[]{:S(2)}) collective-permute-start(bf16[16,128,128]{2,1,0:T(8,128)(2,1)S(1)} %bitcast.144), channel_id=1, source_target_pairs={{0,16},{16,0},{1,17},{17,1},{2,18},{18,2},{3,19},{19,3},{4,20},{20... | collective-permute-start | bytes 1572872 | tf_op jit(solution)/shard_map/ppermute | solution.py:14
  62.3 5.4 %collective-permute-start.19 = (f32[1,72,128]{2,1,0:T(8,128)S(1)}, f32[1,72,128]{2,1,0:T(8,128)S(1)}, u32[]{:S(2)}, u32[]{:S(2)}) collective-permute-start(f32[1,72,128]{2,1,0:T(8,128)S(1)} %slice_bitcast_fusion.10), channel_id=1, source_target_pairs={{0,16},{16,0},{1,17},{17,1},{2,18},{18,2},{3,19},{19,3},{4,20},{20... | collective-permute-start | bytes 110600 | tf_op jit(solution)/shard_map/ppermute | solution.py:14
  63.3 16.6 %collective-permute-start.16 = (bf16[4,128,128]{2,1,0:T(8,128)(2,1)}, bf16[4,128,128]{2,1,0:T(8,128)(2,1)S(1)}, u32[]{:S(2)}, u32[]{:S(2)}) collective-permute-start(bf16[4,128,128]{2,1,0:T(8,128)(2,1)} %get-tuple-element.171.refs_0_), channel_id=1, source_target_pairs={{0,8},{1,9},{2,10},{3,11},{4,12},{5,13},{6,14},{7,15},{8,0},{9,1},... | collective-permute-start | bytes 393224 | tf_op jit(solution)/shard_map/ppermute | solution.py:14
  64.5 15.4 %collective-permute-start.17 = (bf16[4,128,128]{2,1,0:T(8,128)(2,1)}, bf16[4,128,128]{2,1,0:T(8,128)(2,1)S(1)}, u32[]{:S(2)}, u32[]{:S(2)}) collective-permute-start(bf16[4,128,128]{2,1,0:T(8,128)(2,1)} %get-tuple-element.171.refs_0_), channel_id=1, source_target_pairs={{0,4},{1,5},{2,6},{3,7},{4,0},{5,1},{6,2},{7,3},{8,12},{9,13},{10,... | collective-permute-start | bytes 393224 | tf_op jit(solution)/shard_map/ppermute | solution.py:14
  66.3 13.6 %collective-permute-start.18 = (bf16[4,128,128]{2,1,0:T(8,128)(2,1)}, bf16[4,128,128]{2,1,0:T(8,128)(2,1)S(1)}, u32[]{:S(2)}, u32[]{:S(2)}) collective-permute-start(bf16[4,128,128]{2,1,0:T(8,128)(2,1)} %get-tuple-element.171.refs_0_), channel_id=1, source_target_pairs={{0,12},{1,13},{2,14},{3,15},{4,8},{5,9},{6,10},{7,11},{8,4},{9,5},... | collective-permute-start | bytes 393224 | tf_op jit(solution)/shard_map/ppermute | solution.py:14
  67.7 7.9 %collective-permute-start.20 = (f32[72,128]{1,0:T(8,128)S(1)}, f32[72,128]{1,0:T(8,128)S(1)}, u32[]{:S(2)}, u32[]{:S(2)}) collective-permute-start(f32[72,128]{1,0:T(8,128)S(1)} %fusion.26), channel_id=1, source_target_pairs={{0,1},{1,0},{2,3},{3,2},{4,5},{5,4},{6,7},{7,6},{8,9},{9,8},{10,11... | collective-permute-start | bytes 110600 | tf_op jit(solution)/shard_map/ppermute | solution.py:14
  75.6 4.2 %collective-permute-start.21 = (f32[72,128]{1,0:T(8,128)S(1)}, f32[72,128]{1,0:T(8,128)S(1)}, u32[]{:S(2)}, u32[]{:S(2)}) collective-permute-start(f32[72,128]{1,0:T(8,128)S(1)} %add.488), channel_id=1, source_target_pairs={{0,2},{1,3},{2,0},{3,1},{4,6},{5,7},{6,4},{7,5},{8,10},{9,11},{10,... | collective-permute-start | bytes 110600 | tf_op jit(solution)/shard_map/ppermute | solution.py:14
  80.9 9.1 %collective-permute-start.23 = (bf16[4,2,128,128]{3,2,1,0:T(8,128)(2,1)S(1)}, bf16[4,2,128,128]{3,2,1,0:T(8,128)(2,1)S(1)}, u32[]{:S(2)}, u32[]{:S(2)}) collective-permute-start(bf16[4,2,128,128]{3,2,1,0:T(8,128)(2,1)S(1)} %get-tuple-element.183), channel_id=1, source_target_pairs={{0,1},{1,0},{2,3},{3,2},{4,5},{5,4},{6,7},{7,6},{8,9},{9,8},{10,11... | collective-permute-start | bytes 786440 | tf_op jit(solution)/shard_map/ppermute | solution.py:14
  82.0 8.4 %collective-permute-start.22 = (bf16[4,2,128,128]{3,2,1,0:T(8,128)(2,1)S(1)}, bf16[4,2,128,128]{3,2,1,0:T(8,128)(2,1)S(1)}, u32[]{:S(2)}, u32[]{:S(2)}) collective-permute-start(bf16[4,2,128,128]{3,2,1,0:T(8,128)(2,1)S(1)} %get-tuple-element.184), channel_id=1, source_target_pairs={{0,2},{1,3},{2,0},{3,1},{4,6},{5,7},{6,4},{7,5},{8,10},{9,11},{10,... | collective-permute-start | bytes 786440 | tf_op jit(solution)/shard_map/ppermute | solution.py:14
  84.0 4.0 %collective-permute-start.24 = (f32[72,128]{1,0:T(8,128)S(1)}, f32[72,128]{1,0:T(8,128)S(1)}, u32[]{:S(2)}, u32[]{:S(2)}) collective-permute-start(f32[72,128]{1,0:T(8,128)S(1)} %add.489), channel_id=1, source_target_pairs={{0,4},{1,5},{2,6},{3,7},{4,0},{5,1},{6,2},{7,3},{8,12},{9,13},{10,... | collective-permute-start | bytes 110600 | tf_op jit(solution)/shard_map/ppermute | solution.py:14
  90.4 13.8 %collective-permute-start.25 = (bf16[8,2,128,128]{3,2,1,0:T(8,128)(2,1)S(1)}, bf16[8,2,128,128]{3,2,1,0:T(8,128)(2,1)S(1)}, u32[]{:S(2)}, u32[]{:S(2)}) collective-permute-start(bf16[8,2,128,128]{3,2,1,0:T(8,128)(2,1)S(1)} %pad_maximum_fusion.5), channel_id=1, source_target_pairs={{0,1},{1,0},{2,3},{3,2},{4,5},{5,4},{6,7},{7,6},{8,9},{9,8},{10,11... | collective-permute-start | bytes 1572872 | tf_op jit(solution)/shard_map/ppermute | solution.py:14
  92.2 13.6 %collective-permute-start.26 = (bf16[8,2,128,128]{3,2,1,0:T(8,128)(2,1)S(1)}, bf16[8,2,128,128]{3,2,1,0:T(8,128)(2,1)S(1)}, u32[]{:S(2)}, u32[]{:S(2)}) collective-permute-start(bf16[8,2,128,128]{3,2,1,0:T(8,128)(2,1)S(1)} %pad_maximum_fusion.6), channel_id=1, source_target_pairs={{0,2},{1,3},{2,0},{3,1},{4,6},{5,7},{6,4},{7,5},{8,10},{9,11},{10,... | collective-permute-start | bytes 1572872 | tf_op jit(solution)/shard_map/ppermute | solution.py:14
  96.7 5.1 %collective-permute-start.27 = (f32[72,128]{1,0:T(8,128)S(1)}, f32[72,128]{1,0:T(8,128)S(1)}, u32[]{:S(2)}, u32[]{:S(2)}) collective-permute-start(f32[72,128]{1,0:T(8,128)S(1)} %add.490), channel_id=1, source_target_pairs={{0,8},{1,9},{2,10},{3,11},{4,12},{5,13},{6,14},{7,15},{8,0},{9,1},... | collective-permute-start | bytes 110600 | tf_op jit(solution)/shard_map/ppermute | solution.py:14
  105.7 6.8 %collective-permute-start.29 = (f32[72,128]{1,0:T(8,128)S(1)}, f32[72,128]{1,0:T(8,128)S(1)}, u32[]{:S(2)}, u32[]{:S(2)}) collective-permute-start(f32[72,128]{1,0:T(8,128)S(1)} %add.491), channel_id=1, source_target_pairs={{0,16},{16,0},{1,17},{17,1},{2,18},{18,2},{3,19},{19,3},{4,20},{20... | collective-permute-start | bytes 110600 | tf_op jit(solution)/shard_map/ppermute | solution.py:14
  (8 other events, 41.8 us)
